TPU v7x, 128 devices: a whole 4x4x4 slice. The times are simulated.
128 devices in a mesh: neu: 16 (over x_hi, y, core), tri: 8 (over x_lo, z).
Axes of the slice: x: 4 (x_hi: 2, x_lo: 2; x = x_hi * 2 + x_lo), y: 4, z: 4, core: 2. Of those that a mesh axis runs over, the one named last changes fastest.
Arguments:
- spike_counts: bfloat16 [128, 32768, 256], P('tri', 'neu')
- time_factor: bfloat16 [256, 128], replicated, may hold values from -6 to 6
- trial_factor: bfloat16 [128, 128], P('tri'), may hold values from -6 to 6
Outputs:
- neuron_new: float32 [32768, 128], P('neu')
- trial_new: float32 [128, 128], P('tri')
- time_new: float32 [256, 128], replicated
- weights: float32 [128], replicated
All inputs are finite; a program needn't handle non-finite values.
Results may differ from a plain program's by a relative error of at most 0.0004.
Values sent between devices are 32-bit elements; how exact they have to be, the bound alone decides.
No kernel may reach another device: no remote copies, remote signals or barrier semaphores. Data moves between devices by JAX's collectives and lax.ppermute only.
A program may use at most 128 MiB of HBM per device.

v0:
```python
import jax
import jax.numpy as jnp
from jax import lax
from jax.sharding import PartitionSpec as P

highest = lax.Precision.HIGHEST


def solve_right(rhs, system):
    lower = jnp.linalg.cholesky(system)
    return jax.scipy.linalg.cho_solve((lower, True), rhs.T).T


def local_gram(matrix):
    return jnp.dot(matrix.T, matrix, precision=highest, preferred_element_type=jnp.float32)


def column_scales(gram_raw, count):
    return jnp.sqrt(jnp.diagonal(gram_raw) / count + 1e-06)


def body(spike_counts, time_factor, trial_factor):
    trial_rows, neuron_rows, time_bins = spike_counts.shape
    components = time_factor.shape[1]
    neuron_total = neuron_rows * lax.axis_size("neu")
    trial_total = trial_rows * lax.axis_size("tri")
    flattened = spike_counts.reshape(trial_rows * neuron_rows, time_bins)
    gram_time = jnp.dot(time_factor.T, time_factor, preferred_element_type=jnp.float32)
    gram_trial = lax.psum(
        jnp.dot(trial_factor.T, trial_factor, preferred_element_type=jnp.float32), "tri"
    )
    projected = jnp.dot(flattened, time_factor, preferred_element_type=jnp.float32).reshape(
        trial_rows, neuron_rows, components
    )
    neuron_part = jnp.sum(projected * trial_factor.astype(jnp.float32)[:, None, :], axis=0)
    system_neuron = gram_time * gram_trial
    mttkrp_neuron = lax.psum(neuron_part, "tri")
    neuron_raw = solve_right(mttkrp_neuron, system_neuron)
    gram_neuron_raw = lax.psum(local_gram(neuron_raw), "neu")
    scale_neuron = column_scales(gram_neuron_raw, neuron_total)
    neuron_new = neuron_raw / scale_neuron[None, :]
    gram_neuron = gram_neuron_raw / (scale_neuron[:, None] * scale_neuron[None, :])
    neuron_half = neuron_new.astype(jnp.bfloat16)
    contracted = jnp.einsum(
        "kij,ir->krj", spike_counts, neuron_half, preferred_element_type=jnp.float32
    )
    trial_part = jnp.sum(contracted * time_factor.T.astype(jnp.float32)[None, :, :], axis=2)
    mttkrp_trial = lax.psum(trial_part, "neu")
    trial_raw = solve_right(mttkrp_trial, gram_time * gram_neuron)
    gram_trial_raw = lax.psum(local_gram(trial_raw), "tri")
    scale_trial = column_scales(gram_trial_raw, trial_total)
    trial_new = trial_raw / scale_trial[None, :]
    gram_trial_new = gram_trial_raw / (scale_trial[:, None] * scale_trial[None, :])
    khatri_rao = (trial_new[:, None, :] * neuron_new[None, :, :]).astype(jnp.bfloat16)
    khatri_rao = khatri_rao.reshape(trial_rows * neuron_rows, components)
    time_part = lax.dot_general(
        flattened, khatri_rao, (((0,), (0,)), ((), ())), preferred_element_type=jnp.float32
    )
    mttkrp_time = lax.psum(time_part, ("neu", "tri"))
    time_raw = solve_right(mttkrp_time, gram_neuron * gram_trial_new)
    weights = jnp.sqrt(jnp.mean(time_raw * time_raw, axis=0) + 1e-06)
    time_new = time_raw / weights[None, :]
    return (neuron_new, trial_new, time_new, weights)


def solution(mesh):
    return jax.shard_map(
        body,
        mesh=mesh,
        in_specs=(P("tri", "neu", None), P(), P("tri", None)),
        out_specs=(P("neu", None), P("tri", None), P(), P()),
        check_vma=False,
    )
```

profile of v0, /device:TPU:1, one launch (start us, length us, event | category | flops | bytes accessed | tf_op | source)
XLA Modules:
  0.0 607.4 jit_solution(18170398709864389538)
XLA Ops:
  7.2 0.0 all-reduce.12.cloned.1.call-start
  7.2 0.7 convert_element_type.15
  7.9 1.6 fusion.27
  9.5 11.6 %multiply_reduce_fusion = f32[2048,128]{1,0:T(8,128)} fusion(f32[16,128]{1,0:T(8,128)S(1)} %convert_element_type.15, bf16[16,2048,256]{2,1,0:T(8,128)(2,1)} %param.4, bf16[256,128]{1,0:T(8,128)(2,1)} %param.5), kind=kOutput, calls=%fused_computation.3 | convolution fusion | flops 2155610112 | bytes 17899520 | tf_op jit(solution)/shard_map/dot_general | solution.py:32
  21.1 0.0 all-reduce.12.cloned.1.call-update
  21.1 0.2 all-reduce.6.cloned.1.call-start
  21.4 0.1 copy.35
  21.5 75.7 %all-reduce.12.cloned.1.call-done = (f32[2048,128]{1,0:T(8,128)}, f32[128,128]{0,1:T(8,128)}) async-done(((f32[2048,128]{1,0:T(8,128)}, f32[128,128]{0,1:T(8,128)}), (f32[2048,128]{1,0:T(8,128)}, f32[128,128]{0,1:T(8,128)})) %all-reduce.12.cloned.1.call-update) | async-done | bytes 1114128 | tf_op jit(solution)/shard_map/psum | solution.py:37
  97.2 1.1 fusion.26
  98.2 0.1 copy.31
  98.3 11.7 %cholesky.59 = f32[128,128]{1,0:T(8,128)S(1)} custom-call(f32[128,128]{1,0:T(8,128)S(1)} %fusion.24), custom_call_target="Cholesky" | custom-call | tf_op jit(solution)/shard_map/jit(cholesky)/cholesky | solution.py:10
  110.1 0.6 compare_reduce_fusion.2
  110.7 0.7 fusion.6
  111.4 9.8 %custom-call.23 = f32[1,128,128]{1,2,0:T(8,128)S(1)} custom-call(f32[1,128,128]{2,1,0:T(8,128)S(1)} %fusion.6), custom_call_target="InvertDiagBlocksLowerTriangular" | custom-call | tf_op jit(solution)/shard_map/jit(_cho_solve)/triangular_solve | solution.py:11
  121.2 2.3 fusion.22
  123.5 1.0 fusion.20
  124.5 1.6 fusion.28
  126.2 0.3 all-reduce.8.cloned.1.call-start
  126.4 130.3 %all-reduce.6.cloned.1.call-done = f32[128,128]{0,1:T(8,128)} async-done(((f32[128,128]{0,1:T(8,128)}), f32[128,128]{0,1:T(8,128)}) %all-reduce.6.cloned.1.call-update) | async-done | bytes 65552 | tf_op jit(solution)/shard_map/psum | solution.py:39
  256.8 2.0 gather_fusion
  258.8 0.2 divide_bitcast_fusion
  259.0 0.9 fusion.25
  259.9 0.1 copy.34
  260.0 11.7 %cholesky.70 = f32[128,128]{1,0:T(8,128)S(1)} custom-call(f32[128,128]{1,0:T(8,128)S(1)} %fusion.18), custom_call_target="Cholesky" | custom-call | tf_op jit(solution)/shard_map/jit(cholesky)/cholesky | solution.py:10
  271.8 0.6 compare_reduce_fusion.1
  272.4 0.7 fusion.7
  273.1 9.8 %custom-call.24 = f32[1,128,128]{1,2,0:T(8,128)S(1)} custom-call(f32[1,128,128]{2,1,0:T(8,128)S(1)} %fusion.7), custom_call_target="InvertDiagBlocksLowerTriangular" | custom-call | tf_op jit(solution)/shard_map/jit(_cho_solve)/triangular_solve | solution.py:11
  282.9 8.2 %multiply_reduce_fusion.1 = f32[128,16]{0,1:T(8,128)S(1)} fusion(bf16[16,2048,256]{2,1,0:T(8,128)(2,1)} %param.4, f32[128,256]{1,0:T(8,128)S(1)} %copy.35, f32[2048,128]{0,1:T(8,128)S(1)} %divide_bitcast_fusion), kind=kOutput, calls=%fused_computation.7 | convolution fusion | flops 2148792320 | bytes 17965056 | tf_op jit(solution)/shard_map/kij,ir->krj/dot_general | solution.py:44
  291.1 0.1 copy.44
  291.2 63.3 %psum.45 = f32[16,128]{0,1:T(8,128)S(1)} all-reduce(f32[16,128]{0,1:T(8,128)S(1)} %bitcast.71), channel_id=1, replica_groups=mesh['neu'=16,'tri'=8] {'neu'}, use_global_device_ids=true, to_apply=%region_7.9 | all-reduce | flops 2048 | bytes 16384 | tf_op jit(solution)/shard_map/psum | solution.py:48
  354.5 0.2 fusion.16
  354.8 0.2 fusion.14
  355.0 1.0 fusion.29
  356.0 0.3 all-reduce.10.cloned.1.call-start
  356.3 1.3 copy.39
  357.6 72.2 %all-reduce.8.cloned.1.call-done = f32[128,128]{0,1:T(8,128)} async-done(((f32[128,128]{0,1:T(8,128)}), f32[128,128]{0,1:T(8,128)}) %all-reduce.8.cloned.1.call-update) | async-done | bytes 65552 | tf_op jit(solution)/shard_map/psum | solution.py:50
  429.8 1.9 gather_fusion.1
  431.8 0.9 divide_multiply_fusion
  432.8 0.1 copy.38
  432.9 11.7 %cholesky.81 = f32[128,128]{1,0:T(8,128)S(1)} custom-call(f32[128,128]{1,0:T(8,128)S(1)} %fusion.13), custom_call_target="Cholesky" | custom-call | tf_op jit(solution)/shard_map/jit(cholesky)/cholesky | solution.py:10
  444.6 0.6 compare_reduce_fusion
  445.3 8.8 %fusion.3 = f32[256,128]{0,1:T(8,128)} fusion(bf16[16,2048,256]{2,1,0:T(8,128)(2,1)} %param.4, f32[2048,128]{0,1:T(8,128)S(1)} %divide_bitcast_fusion, f32[16,128]{1,0:T(8,128)S(1)} %divide_bitcast_fusion.1), kind=kOutput, calls=%fused_computation.8 | convolution fusion | flops 2155872256 | bytes 17965056 | tf_op jit(solution)/shard_map/dot_general | solution.py:56
  454.1 0.7 fusion.8
  454.8 9.8 %custom-call.25 = f32[1,128,128]{1,2,0:T(8,128)S(1)} custom-call(f32[1,128,128]{2,1,0:T(8,128)S(1)} %fusion.8), custom_call_target="InvertDiagBlocksLowerTriangular" | custom-call | tf_op jit(solution)/shard_map/jit(_cho_solve)/triangular_solve | solution.py:11
  464.6 134.0 %all-reduce.10.cloned.1.call-done = f32[256,128]{0,1:T(8,128)} async-done(((f32[256,128]{0,1:T(8,128)}), f32[256,128]{0,1:T(8,128)}) %all-reduce.10.cloned.1.call-update) | async-done | bytes 131088 | tf_op jit(solution)/shard_map/psum | solution.py:59
  598.5 1.2 fusion.11
  599.8 0.4 multiply_reduce_fusion.2
  600.2 0.7 broadcast_divide_fusion
  (23 shorter events, 0.3 us)
Async XLA Ops:
  7.2 14.2 %copy-start.1 = (bf16[256,128]{1,0:T(8,128)(2,1)S(1)}, bf16[256,128]{1,0:T(8,128)(2,1)}, u32[]{:S(2)}) copy-start(bf16[256,128]{1,0:T(8,128)(2,1)} %param.5) | copy-start | bytes 196612
  7.2 90.0 %all-reduce.12.cloned.1.call-start = ((), (), s32[]{:S(2)}) async-start(), calls=%async_computation.3 | async-start | bytes 2228224 | tf_op jit(solution)/shard_map/psum | solution.py:37
  21.1 235.7 %all-reduce.6.cloned.1.call-start = ((), (), s32[]{:S(2)}) async-start(), calls=%async_computation | async-start | bytes 131072 | tf_op jit(solution)/shard_map/psum | solution.py:39
  126.2 303.7 %all-reduce.8.cloned.1.call-start = ((), (), s32[]{:S(2)}) async-start(), calls=%async_computation.1 | async-start | bytes 131072 | tf_op jit(solution)/shard_map/psum | solution.py:50
  256.8 175.0 %copy-start = (f32[128,128]{0,1:T(8,128)S(1)}, f32[128,128]{0,1:T(8,128)}, u32[]{:S(2)}) copy-start(f32[128,128]{0,1:T(8,128)} %all-reduce.6.cloned.1.call-done) | copy-start | bytes 196612
  356.0 242.6 %all-reduce.10.cloned.1.call-start = ((), (), s32[]{:S(2)}) async-start(), calls=%async_computation.2 | async-start | bytes 262144 | tf_op jit(solution)/shard_map/psum | solution.py:59
  431.8 169.1 %copy-start.2 = (f32[16,128]{1,0:T(8,128)}, f32[16,128]{1,0:T(8,128)S(1)}, u32[]{:S(2)}) copy-start(f32[16,128]{1,0:T(8,128)S(1)} %divide_bitcast_fusion.1) | copy-start | bytes 24580
  600.2 0.7 copy-start.3
Sparse Core Ops, SparseCore 0:
  21.2 75.8 all-reduce.11
  126.3 130.4 all-reduce.5
  356.1 73.6 all-reduce.7
  454.2 144.2 all-reduce.9
where the time goes:
time: 608 us; the launch traced here: 607 us
  waiting for transfers between devices  412 us (68%)
  other arithmetic  72.1 us (12%)
  blocking collectives  63.3 us (10%)
  matrix products  39.1 us (6%)
  between operations  14 us (2%)
    psum x1, waiting for transfers between devices, body(): mttkrp_time = lax.psum(time_part, ('neu', 'tri'))  134 us
    psum x1, waiting for transfers between devices, body(): gram_neuron_raw = lax.psum(local_gram(neuron_raw), 'neu')  130 us
    psum x1, waiting for transfers between devices, body(): mttkrp_neuron = lax.psum(neuron_part, 'tri')  75.7 us
    psum x1, waiting for transfers between devices, body(): gram_trial_raw = lax.psum(local_gram(trial_raw), 'tri')  72.2 us
    psum x1, blocking collectives, body(): mttkrp_trial = lax.psum(trial_part, 'neu')  63.3 us
    another operation x9, other arithmetic, solve_right(): lower = jnp.linalg.cholesky(system)  37.2 us
    another operation x6, other arithmetic, solve_right(): return jax.scipy.linalg.cho_solve((lower, True), rhs.T).T  31.4 us
  transfers between devices with their start and end apart: 4, of which 4 were waited for; matrix products, arithmetic and copies ran while one was open for 2% of the time, Pallas kernels for 0%

commit v1 on v0

v1 whole, which is shorter than its diff:
```python
import jax
import jax.numpy as jnp
from jax import lax
from jax.experimental import pallas as pl
from jax.experimental.pallas import tpu as pltpu
from jax.sharding import PartitionSpec as P

f32 = jnp.float32
bf16 = jnp.bfloat16
highest = lax.Precision.HIGHEST
WHOLE = pl.BlockSpec(memory_space=pltpu.VMEM)
MIB = 1 << 20
AHEAD = 3


def call(kernel, outs, name, in_specs, limit=12, scratch=()):
    return pl.pallas_call(
        kernel,
        in_specs=in_specs,
        out_specs=[WHOLE] * len(outs),
        out_shape=outs,
        scratch_shapes=scratch,
        compiler_params=pltpu.CompilerParams(vmem_limit_bytes=limit * MIB),
        name=name,
    )


def array(*shape):
    return jax.ShapeDtypeStruct(shape, f32)


def dot(a, b, dims=((1,), (0,))):
    return lax.dot_general(a, b, (dims, ((), ())), precision=highest, preferred_element_type=f32)


def identity(n):
    rows = lax.broadcasted_iota(jnp.int32, (n, n), 0)
    columns = lax.broadcasted_iota(jnp.int32, (n, n), 1)
    return jnp.where(rows == columns, 1.0, 0.0).astype(f32)


def row_norm(matrix):
    return jnp.max(jnp.sum(jnp.abs(matrix), axis=1, keepdims=True))


def inverse(system, scaled_ref, approx_ref, error_ref):
    n = system.shape[0]
    eye = identity(n)
    diagonal = system * eye
    left = 1.0 / jnp.sqrt(jnp.sum(diagonal, axis=1, keepdims=True))
    right = 1.0 / jnp.sqrt(jnp.sum(diagonal, axis=0, keepdims=True))
    scaled = system * left * right
    bound = row_norm(scaled)
    step = jnp.where(bound < 1.98, 1.0, 1.96 / bound)
    error = eye - step * scaled
    scaled_ref[...] = scaled
    approx_ref[...] = step * (eye + error)
    error = dot(error, error)
    error_ref[...] = error

    def going(state):
        count, norm = state
        return (norm > 1e-2) & (count < 40)

    def square(state):
        error = error_ref[...]
        approx = approx_ref[...]
        approx_ref[...] = approx + dot(approx, error)
        error = dot(error, error)
        error_ref[...] = error
        return state[0] + 1, row_norm(error)

    lax.while_loop(going, square, (0, row_norm(error)))

    def refining(state):
        count, norm = state
        return (norm > 5e-4) & (count < 6)

    def refine(state):
        approx = approx_ref[...]
        residual = eye - dot(scaled_ref[...], approx)
        approx_ref[...] = approx + dot(approx, residual)
        return state[0] + 1, row_norm(residual)

    lax.while_loop(refining, refine, (0, jnp.float32(1.0)))
    approx = approx_ref[...]
    return approx * left * right


def neuron_pass(spikes_hbm, time_ref, trial_ref, spikes_ref, projected_ref, part_ref, sems):
    trials = spikes_ref.shape[0]
    blocks, extended, _ = part_ref.shape
    rows = extended - trials
    trial = trial_ref[...].astype(f32)
    copies = []
    for b in range(blocks):
        span = pl.ds(b * rows, rows)
        copies.append(
            pltpu.make_async_copy(spikes_hbm.at[:, span, :], spikes_ref.at[:, span, :], sems.at[b])
        )
    for b in range(min(AHEAD, blocks)):
        copies[b].start()
    for b in range(blocks):
        copies[b].wait()
        if b + AHEAD < blocks:
            copies[b + AHEAD].start()
        span = pl.ds(b * rows, rows)
        total = None
        for k in range(trials):
            projected = jnp.dot(spikes_ref[k, span, :], time_ref[...], preferred_element_type=f32)
            projected_ref[k, span, :] = projected
            term = projected * trial[k : k + 1, :]
            total = term if total is None else total + term
        part_ref[b, 0:rows, :] = total
        part_ref[b, rows:extended, :] = trial


def sum_blocks(parts_ref, copies_ref, trial_ref):
    blocks, rows, _ = copies_ref.shape
    extended = parts_ref.shape[1]
    trials = extended - rows
    total = parts_ref[0, 0:rows, :]
    for b in range(1, blocks):
        total = total + parts_ref[b, 0:rows, :]
    for b in range(blocks):
        copies_ref[b] = total
        trial_ref[b * trials : (b + 1) * trials, :] = parts_ref[b, rows:extended, :]


def first_system(time_ref, trial_ref, inverse_ref, gram_time_ref, *work):
    across = (((0,), (0,)), ((), ()))
    trial = trial_ref[...].astype(bf16)
    gram_time = lax.dot_general(time_ref[...], time_ref[...], across, preferred_element_type=f32)
    gram_trial = lax.dot_general(trial, trial, across, preferred_element_type=f32)
    gram_time_ref[...] = gram_time
    inverse_ref[...] = inverse(gram_time * gram_trial, *work)


def neuron_solve(mttkrp_ref, inverse_ref, raw_ref, gram_ref):
    raw = dot(mttkrp_ref[...], inverse_ref[...])
    raw_ref[...] = raw
    gram_ref[...] = dot(raw, raw, ((0,), (0,)))


def trial_pass(count, grams_ref, raw_ref, projected_ref, new_ref, flipped_ref, gram_ref, part_ref, half_ref):
    trials, rows, components = projected_ref.shape
    gram_raw = jnp.sum(grams_ref[...], axis=0)
    diagonal = gram_raw * identity(components)
    scale = jnp.sqrt(jnp.sum(diagonal, axis=0, keepdims=True) / count + 1e-06)
    scale_down = jnp.sqrt(jnp.sum(diagonal, axis=1, keepdims=True) / count + 1e-06)
    gram_ref[...] = gram_raw / (scale * scale_down)
    new = raw_ref[...] / scale
    new_ref[...] = new
    flipped_ref[...] = new.T
    half_ref[...] = new.astype(bf16).astype(f32)
    block = 64

    def step(b, totals):
        span = pl.ds(pl.multiple_of(b * block, block), block)
        half = half_ref[span, :]
        return [
            totals[k]
            + jnp.sum((projected_ref[k, span, :] * half).reshape(block // 8, 8, components), axis=0)
            for k in range(trials)
        ]

    totals = lax.fori_loop(0, rows // block, step, [jnp.zeros((8, components), f32)] * trials)
    part = jnp.concatenate([jnp.sum(total, axis=0, keepdims=True) for total in totals], axis=0)
    for d in range(part_ref.shape[0]):
        part_ref[d] = part


def second_system(gram_time_ref, gram_ref, inverse_ref, *work):
    inverse_ref[...] = inverse(gram_time_ref[...] * gram_ref[...], *work)


def time_pass(
    here_ref, ours_ref, theirs_ref, inverse_ref, gram_neuron_ref, flipped_ref, spikes_ref,
    trial_ref, system_ref, part_ref, table_ref,
):
    trials, rows, bins = spikes_ref.shape
    components = inverse_ref.shape[0]
    raw = dot(ours_ref[...] + theirs_ref[...], inverse_ref[...])
    gram_raw = dot(raw, raw, ((0,), (0,)))
    diagonal = gram_raw * identity(components)
    count = raw.shape[0]
    scale = jnp.sqrt(jnp.sum(diagonal, axis=0, keepdims=True) / count + 1e-06)
    scale_down = jnp.sqrt(jnp.sum(diagonal, axis=1, keepdims=True) / count + 1e-06)
    system_ref[...] = gram_neuron_ref[...] * (gram_raw / (scale * scale_down))
    table_ref[...] = raw / scale
    own = table_ref[pl.ds(pl.multiple_of(here_ref[0] * trials, trials), trials), :]
    trial_ref[...] = own
    columns = own.T
    total = None
    for k in range(trials):
        khatri_rao = (flipped_ref[...] * columns[:, k : k + 1]).astype(bf16)
        term = jnp.dot(khatri_rao, spikes_ref[k], preferred_element_type=f32)
        total = term if total is None else total + term
    part_ref[...] = total


def third_system(system_ref, inverse_ref, *work):
    inverse_ref[...] = inverse(system_ref[...], *work)


def time_solve(mttkrp_ref, inverse_ref, time_ref, weights_ref):
    raw = dot(inverse_ref[...], mttkrp_ref[...]).T
    weights = jnp.sqrt(jnp.mean(raw * raw, axis=0, keepdims=True) + 1e-06)
    weights_ref[...] = weights
    time_ref[...] = raw / weights


def body(spike_counts, time_factor, trial_factor):
    trials, rows, bins = spike_counts.shape
    components = time_factor.shape[1]
    neu, tri = lax.axis_size("neu"), lax.axis_size("tri")
    block = rows // tri
    half = neu // 2
    both = ("neu", "tri")
    swap = [(i, i ^ 1) for i in range(neu)]
    any_memory = pl.BlockSpec(memory_space=pl.ANY)

    spikes, projected, part = call(
        neuron_pass,
        [
            pltpu.VMEM(spike_counts.shape, bf16),
            pltpu.VMEM((trials, rows, components), f32),
            array(tri, block + trials, components),
        ],
        "neuron_pass",
        [any_memory, WHOLE, WHOLE],
        16,
        [pltpu.SemaphoreType.DMA((tri,))],
    )(spike_counts, time_factor, trial_factor)
    parts = lax.all_to_all(part, "tri", 0, 0)
    copies, trial_old = call(
        sum_blocks, [array(tri, block, components), array(tri * trials, components)], "sum_blocks", [WHOLE]
    )(parts)
    mttkrp_neuron = lax.all_to_all(copies, "tri", 0, 0).reshape(rows, components)
    square = array(components, components)
    work = [pltpu.VMEM((components, components), f32)] * 3
    inverse_one, gram_time = call(first_system, [square, square], "first_system", [WHOLE] * 2, 12, work)(
        time_factor, trial_old
    )
    raw, gram_part = call(neuron_solve, [array(rows, components), square], "neuron_solve", [WHOLE] * 2)(
        mttkrp_neuron, inverse_one
    )
    gram_part = gram_part + lax.ppermute(gram_part, "neu", swap)
    groups = [list(range(c, neu, 2)) for c in range(2)]
    grams = lax.all_to_all(
        jnp.broadcast_to(gram_part[None], (half, components, components)), "neu", 0, 0, axis_index_groups=groups
    )
    neuron_new, flipped, gram_neuron, trial_part = call(
        lambda *refs: trial_pass(neu * rows, *refs),
        [
            array(rows, components),
            array(components, rows),
            square,
            array(half * tri, trials, components),
        ],
        "trial_pass",
        [WHOLE] * 3,
        12,
        [pltpu.VMEM((rows, components), f32)],
    )(grams, raw, projected)
    groups = [[n * tri + t for n in range(c, neu, 2) for t in range(tri)] for c in range(2)]
    gathered = lax.all_to_all(trial_part, both, 0, 0, axis_index_groups=groups)
    (inverse_two,) = call(second_system, [square], "second_system", [WHOLE] * 2, 12, work)(gram_time, gram_neuron)
    ours = jnp.sum(gathered.reshape(half, tri * trials, components), axis=0)
    theirs = lax.ppermute(ours, "neu", swap)
    here = lax.axis_index("tri").astype(jnp.int32).reshape(1)
    trial_new, system_three, time_part = call(
        time_pass,
        [array(trials, components), square, array(components, bins)],
        "time_pass",
        [pl.BlockSpec(memory_space=pltpu.SMEM)] + [WHOLE] * 6,
        12,
        [pltpu.VMEM((tri * trials, components), f32)],
    )(here, ours, theirs, inverse_two, gram_neuron, flipped, spikes)
    pieces = lax.all_to_all(time_part.reshape(neu * tri, components // (neu * tri), bins), both, 0, 0)
    (inverse_three,) = call(third_system, [square], "third_system", [WHOLE], 12, work)(system_three)
    piece = jnp.sum(pieces, axis=0, keepdims=True)
    mttkrp_time = lax.all_to_all(jnp.broadcast_to(piece, pieces.shape), both, 0, 0).reshape(components, bins)
    time_new, weights = call(time_solve, [array(bins, components), array(1, components)], "time_solve", [WHOLE] * 2)(
        mttkrp_time, inverse_three
    )
    return neuron_new, trial_new, time_new, weights[0]


def solution(mesh):
    return jax.shard_map(
        body,
        mesh=mesh,
        in_specs=(P("tri", "neu", None), P(), P("tri", None)),
        out_specs=(P("neu", None), P("tri", None), P(), P()),
        check_vma=False,
    )
```

time: 608 us -> 154 us (0.25)
  waiting for transfers between devices: 412 us -> 16 us
  other arithmetic: 72.1 us -> 0.19 us
  matrix products: 39.1 us -> 0 us
  Pallas kernels: 0 us -> 27.3 us
  local copies, waits for them, and re-layouts: 5.75 us -> 25.4 us
  starting transfers between devices: 0.83 us -> 15 us
  between operations: 14 us -> 0.75 us
    psum x4 -> x0, waiting for transfers between devices: 412 us -> none  [the longest x1 134 us: body(): mttkrp_time = lax.psum(time_part, ('neu', 'tri'))]
    all_to_all x0 -> x4, blocking collectives: none -> 68.7 us  [the longest x1 21.8 us: body(): parts = lax.all_to_all(part, 'tri', 0, 0)]
    another operation x15 -> x0, other arithmetic: 68.6 us -> none  [the longest x9 37.2 us: solve_right(): lower = jnp.linalg.cholesky(system)]
    psum x1 -> x0, blocking collectives: 63.3 us -> none  [body(): mttkrp_trial = lax.psum(trial_part, 'neu')]
    dot_general x7 -> x0, matrix products: 33.8 us -> none  [the longest x1 11.6 us: body(): jnp.dot(flattened, time_factor, preferred_element_type=jnp.float32)]
    pallas_call x0 -> x9, Pallas kernels: none -> 27.3 us  [the longest x1 7.29 us: body(): call(neuron_pass, [pltpu.VMEM(spike_counts.shape, bf16), pltpu.VMEM((tria...]
    unnamed x10 -> x15, local copies, waits for them, and re-layouts: 1.43 us -> 24.5 us
    all_to_all x0 -> x2, waiting for transfers between devices: none -> 15.1 us  [the longest x1 8.85 us: body(): lax.all_to_all(copies, 'tri', 0, 0).reshape(rows, components)]
  transfers between devices with their start and end apart: 4 -> 4, of which waited for: 4 -> 3; matrix products, arithmetic and copies ran while one was open for 2% -> 0% of each run, Pallas kernels for 0% -> 6%
where the time goes in v1:
time: 154 us; the launch traced here: 153 us
  blocking collectives  68.7 us (45%)
  Pallas kernels  27.3 us (18%)
  local copies, waits for them, and re-layouts  25.4 us (16%)
  waiting for transfers between devices  16 us (10%)
  starting transfers between devices  15 us (10%)
    unnamed x15, local copies, waits for them, and re-layouts  24.5 us
    all_to_all x1, blocking collectives, body(): parts = lax.all_to_all(part, 'tri', 0, 0)  21.8 us
    all_to_all x1, blocking collectives, body(): gathered = lax.all_to_all(trial_part, both, 0, 0, axis_index_groups=groups)  17.5 us
    all_to_all x1, blocking collectives, body(): lax.all_to_all(jnp.broadcast_to(gram_part[None], (half, components, compo...  16.2 us
    all_to_all x1, blocking collectives, body(): lax.all_to_all(time_part.reshape(neu * tri, components // (neu * tri), bi...  13.2 us
    all_to_all x1, waiting for transfers between devices, body(): lax.all_to_all(copies, 'tri', 0, 0).reshape(rows, components)  8.85 us
    pallas_call x1, Pallas kernels, body(): call(neuron_pass, [pltpu.VMEM(spike_counts.shape, bf16), pltpu.VMEM((tria...  7.29 us
    all_to_all x1, waiting for transfers between devices, body(): lax.all_to_all(jnp.broadcast_to(piece, pieces.shape), both, 0, 0)  6.26 us
  transfers between devices with their start and end apart: 4, of which 3 were waited for; matrix products, arithmetic and copies ran while one was open for 0% of the time, Pallas kernels for 6%

profile of v1, /device:TPU:1, one launch (start us, length us, event | category | flops | bytes accessed | tf_op | source)
XLA Modules:
  0.0 153.4 jit_solution(1621766034202295574)
XLA Ops:
  0.6 0.0 copy-start.4
  0.6 0.8 copy-done.4
  1.5 0.0 copy-start.6
  1.5 0.7 copy-done.6
  2.2 0.0 copy-start.5
  2.2 7.3 %neuron_pass.1 = (bf16[16,2048,256]{2,1,0:T(8,128)(2,1)S(1)}, f32[16,2048,128]{2,1,0:T(8,128)S(1)}, f32[8,272,128]{2,1,0:T(8,128)S(1)}) custom-call(bf16[16,2048,256]{2,1,0:T(8,128)(2,1)} %spikes_hbm.1, bf16[256,128]{1,0:T(8,128)(2,1)S(1)} %copy-done.4, bf16[16,128]{1,0:T(8,128)(2,1)S(1)} %copy-done.6), custom_call_target="tpu_custom_call" | custom-call | tf_op jit(solution)/shard_map/neuron_pass/pallas_call | solution.py:223
  9.5 0.0 copy-start
  9.5 5.7 %copy-done = bf16[16,2048,256]{2,1,0:T(8,128)(2,1)} copy-done((bf16[16,2048,256]{2,1,0:T(8,128)(2,1)}, bf16[16,2048,256]{2,1,0:T(8,128)(2,1)S(1)}, u32[]{:S(2)}) %copy-start) | copy-done | bytes 16777240
  15.2 0.0 copy-start.2
  15.2 5.7 %copy-done.2 = f32[16,2048,128]{2,1,0:T(8,128)} copy-done((f32[16,2048,128]{2,1,0:T(8,128)}, f32[16,2048,128]{2,1,0:T(8,128)S(1)}, u32[]{:S(2)}) %copy-start.2) | copy-done | bytes 16777240
  20.9 21.8 %all_to_all.30.parts_ref = f32[8,272,128]{2,1,0:T(8,128)S(1)} all-to-all(f32[8,272,128]{2,1,0:T(8,128)S(1)} %get-tuple-element.22), channel_id=1, replica_groups=mesh['neu'=16,'tri'=8] {'tri'}, dimensions={0} | all-to-all | bytes 2228224 | tf_op jit(solution)/shard_map/all_to_all | solution.py:235
  42.8 1.1 sum_blocks.1
  43.8 3.6 %all-to-all-start.1 = ((f32[8,256,128]{2,1,0:T(8,128)}), f32[8,256,128]{2,1,0:T(8,128)S(1)}, u32[]{:S(2)}, u32[]{:S(2)}) async-start(f32[8,256,128]{2,1,0:T(8,128)} %get-tuple-element.23), calls=%async_computation.1 | async-start | bytes 2097152 | tf_op jit(solution)/shard_map/all_to_all | solution.py:239
  47.4 0.0 copy-done.5
  47.4 2.5 %first_system.1 = (f32[128,128]{1,0:T(8,128)S(1)}, f32[128,128]{1,0:T(8,128)S(1)}) custom-call(bf16[256,128]{1,0:T(8,128)(2,1)S(1)} %copy-done.5, f32[128,128]{1,0:T(8,128)S(1)} %get-tuple-element.24.trial_ref), custom_call_target="tpu_custom_call" | custom-call | tf_op jit(solution)/shard_map/first_system/pallas_call | solution.py:242
  49.9 8.8 %all-to-all-done.1 = f32[8,256,128]{2,1,0:T(8,128)S(1)} async-done(((f32[8,256,128]{2,1,0:T(8,128)}), f32[8,256,128]{2,1,0:T(8,128)S(1)}, u32[]{:S(2)}, u32[]{:S(2)}) %all-to-all-start.1) | async-done | bytes 1048608 | tf_op jit(solution)/shard_map/all_to_all | solution.py:239
  58.8 3.4 %neuron_solve.1 = (f32[2048,128]{1,0:T(8,128)S(1)}, f32[128,128]{1,0:T(8,128)S(1)}) custom-call(f32[2048,128]{1,0:T(8,128)S(1)} %bitcast.10, f32[128,128]{1,0:T(8,128)S(1)} %get-tuple-element.25.inverse_ref), custom_call_target="tpu_custom_call" | custom-call | tf_op jit(solution)/shard_map/neuron_solve/pallas_call | solution.py:245
  62.2 4.4 %collective-permute-start = (f32[128,128]{1,0:T(8,128)S(1)}, f32[128,128]{1,0:T(8,128)S(1)}, u32[]{:S(2)}, u32[]{:S(2)}) collective-permute-start(f32[128,128]{1,0:T(8,128)S(1)} %get-tuple-element.26), channel_id=1, source_target_pairs={{0,8},{8,0},{16,24},{24,16},{32,40},{40,32},{48,56},{56,48},{64,72... | collective-permute-start | bytes 196616 | tf_op jit(solution)/shard_map/ppermute | solution.py:248
  66.5 0.9 collective-permute-done
  67.5 16.2 %all_to_all.31.refs_0_ = f32[8,128,128]{2,1,0:T(8,128)S(1)} all-to-all(f32[8,128,128]{2,1,0:T(8,128)S(1)} %broadcast_in_dim.4), channel_id=1, replica_groups={{0,16,32,48,64,80,96,112},{8,24,40,56,72,88,104,120},{1,17,33,49,65,81,..., dimensions={0} | all-to-all | bytes 1048576 | tf_op jit(solution)/shard_map/all_to_all | solution.py:250
  83.7 0.0 copy-start.3
  83.7 5.8 %copy-done.3 = f32[16,2048,128]{2,1,0:T(8,128)S(1)} copy-done((f32[16,2048,128]{2,1,0:T(8,128)S(1)}, f32[16,2048,128]{2,1,0:T(8,128)}, u32[]{:S(2)}) %copy-start.3) | copy-done | bytes 16777240
  89.5 2.8 %trial_pass.1 = (f32[2048,128]{1,0:T(8,128)}, f32[128,2048]{1,0:T(8,128)S(1)}, f32[128,128]{1,0:T(8,128)S(1)}, f32[64,16,128]{2,1,0:T(8,128)S(1)}) custom-call(f32[8,128,128]{2,1,0:T(8,128)S(1)} %all_to_all.31.refs_0_, f32[2048,128]{1,0:T(8,128)S(1)} %get-tuple-element.27.refs_1_, f32[16,2048,128]{2,1,0:T(8,128)S(1)} %copy-done.3), custom_call_target="tpu_custom_call" | custom-call | tf_op jit(solution)/shard_map/trial_pass/pallas_call | solution.py:253
  92.2 17.5 %all_to_all.32 = f32[64,16,128]{2,1,0:T(8,128)S(1)} all-to-all(f32[64,16,128]{2,1,0:T(8,128)S(1)} %get-tuple-element.30), channel_id=1, replica_groups={{0,1,2,3,4,5,6,7,16,17,18,19,20,21,22,23,32,33,34,35,36,37,38,39,48,49,..., dimensions={0} | all-to-all | bytes 1048576 | tf_op jit(solution)/shard_map/all_to_all | solution.py:267
  109.8 2.8 %collective-permute-start.1 = (f32[128,128]{1,0:T(8,128)S(1)}, f32[128,128]{1,0:T(8,128)S(1)}, u32[]{:S(2)}, u32[]{:S(2)}) collective-permute-start(f32[128,128]{1,0:T(8,128)S(1)} %bitcast_reduce_fusion.ours_ref), channel_id=1, source_target_pairs={{0,8},{8,0},{16,24},{24,16},{32,40},{40,32},{48,56},{56,48},{64,72... | collective-permute-start | bytes 196616 | tf_op jit(solution)/shard_map/ppermute | solution.py:270
  112.6 2.5 %second_system.1.inverse_ref = f32[128,128]{1,0:T(8,128)S(1)} custom-call(f32[128,128]{1,0:T(8,128)S(1)} %get-tuple-element.31.gram_time_ref, f32[128,128]{1,0:T(8,128)S(1)} %get-tuple-element.32.gram_ref.gram_neuron_ref), custom_call_target="tpu_custom_call" | custom-call | tf_op jit(solution)/shard_map/second_system/pallas_call | solution.py:268
  115.0 0.0 collective-permute-done.1.theirs_ref
  115.0 0.0 copy-start.1
  115.0 5.8 %copy-done.1 = bf16[16,2048,256]{2,1,0:T(8,128)(2,1)S(1)} copy-done((bf16[16,2048,256]{2,1,0:T(8,128)(2,1)S(1)}, bf16[16,2048,256]{2,1,0:T(8,128)(2,1)}, u32[]{:S(2)}) %copy-start.1) | copy-done | bytes 16777240
  120.8 3.0 %time_pass.1 = (f32[16,128]{1,0:T(8,128)}, f32[128,128]{1,0:T(8,128)S(1)}, f32[128,256]{1,0:T(8,128)S(1)}) custom-call(s32[1]{0:T(128)} %bitcast.1.here_ref, f32[128,128]{1,0:T(8,128)S(1)} %bitcast_reduce_fusion.ours_ref, f32[128,128]{1,0:T(8,128)S(1)} %collective-permute-done.1.theirs_ref, f32[128,128]{1,0:T(8,128)S(1)} %second_system.1.inverse_ref, ...), custom_call_target="tpu_custom_call" | custom-call | tf_op jit(solution)/shard_map/time_pass/pallas_call | solution.py:272
  123.8 0.1 copy.7
  124.0 13.2 %all_to_all.33 = f32[128,1,256]{2,1,0:T(1,128)S(1)} all-to-all(f32[128,1,256]{2,1,0:T(1,128)S(1)} %copy.7), channel_id=1, replica_groups=mesh['neu'=16,'tri'=8] {'neu','tri'}, dimensions={0} | all-to-all | bytes 262144 | tf_op jit(solution)/shard_map/all_to_all | solution.py:280
  137.1 0.2 reduce_sum.19
  137.3 0.7 broadcast_in_dim.5
  138.0 4.3 %all-to-all-start.5 = ((f32[128,1,256]{2,1,0:T(1,128)}), f32[128,1,256]{2,1,0:T(1,128)S(1)}, u32[]{:S(2)}, u32[]{:S(2)}) async-start(f32[128,1,256]{2,1,0:T(1,128)} %broadcast_in_dim.5), calls=%async_computation.5 | async-start | bytes 262144 | tf_op jit(solution)/shard_map/all_to_all | solution.py:283
  142.3 3.8 %third_system.1.inverse_ref = f32[128,128]{1,0:T(8,128)S(1)} custom-call(f32[128,128]{1,0:T(8,128)S(1)} %get-tuple-element.37.system_ref), custom_call_target="tpu_custom_call" | custom-call | tf_op jit(solution)/shard_map/third_system/pallas_call | solution.py:281
  146.1 6.3 %all-to-all-done.5 = f32[128,1,256]{2,1,0:T(1,128)S(1)} async-done(((f32[128,1,256]{2,1,0:T(1,128)}), f32[128,1,256]{2,1,0:T(1,128)S(1)}, u32[]{:S(2)}, u32[]{:S(2)}) %all-to-all-start.5) | async-done | bytes 131104 | tf_op jit(solution)/shard_map/all_to_all | solution.py:283
  152.4 1.0 time_solve.1
  (4 shorter events, 0.1 us)
Async XLA Ops:
  0.6 0.8 copy-start.4
  1.5 0.7 copy-start.6
  2.2 45.2 %copy-start.5 = (bf16[256,128]{1,0:T(8,128)(2,1)S(1)}, bf16[256,128]{1,0:T(8,128)(2,1)}, u32[]{:S(2)}) copy-start(bf16[256,128]{1,0:T(8,128)(2,1)} %time_ref.3) | copy-start | bytes 196612
  9.5 5.7 %copy-start = (bf16[16,2048,256]{2,1,0:T(8,128)(2,1)}, bf16[16,2048,256]{2,1,0:T(8,128)(2,1)S(1)}, u32[]{:S(2)}) copy-start(bf16[16,2048,256]{2,1,0:T(8,128)(2,1)S(1)} %get-tuple-element.34.spikes_ref) | copy-start | bytes 50331652
  15.2 5.7 %copy-start.2 = (f32[16,2048,128]{2,1,0:T(8,128)}, f32[16,2048,128]{2,1,0:T(8,128)S(1)}, u32[]{:S(2)}) copy-start(f32[16,2048,128]{2,1,0:T(8,128)S(1)} %get-tuple-element.28.refs_2_) | copy-start | bytes 50331652
  43.8 14.9 %all-to-all-start.1 = ((f32[8,256,128]{2,1,0:T(8,128)}), f32[8,256,128]{2,1,0:T(8,128)S(1)}, u32[]{:S(2)}, u32[]{:S(2)}) async-start(f32[8,256,128]{2,1,0:T(8,128)} %get-tuple-element.23), calls=%async_computation.1 | async-start | bytes 2097152 | tf_op jit(solution)/shard_map/all_to_all | solution.py:239
  62.2 5.3 %collective-permute-start = (f32[128,128]{1,0:T(8,128)S(1)}, f32[128,128]{1,0:T(8,128)S(1)}, u32[]{:S(2)}, u32[]{:S(2)}) collective-permute-start(f32[128,128]{1,0:T(8,128)S(1)} %get-tuple-element.26), channel_id=1, source_target_pairs={{0,8},{8,0},{16,24},{24,16},{32,40},{40,32},{48,56},{56,48},{64,72... | collective-permute-start | bytes 196616 | tf_op jit(solution)/shard_map/ppermute | solution.py:248
  83.7 5.8 %copy-start.3 = (f32[16,2048,128]{2,1,0:T(8,128)S(1)}, f32[16,2048,128]{2,1,0:T(8,128)}, u32[]{:S(2)}) copy-start(f32[16,2048,128]{2,1,0:T(8,128)} %copy-done.2) | copy-start | bytes 50331652
  109.8 5.2 %collective-permute-start.1 = (f32[128,128]{1,0:T(8,128)S(1)}, f32[128,128]{1,0:T(8,128)S(1)}, u32[]{:S(2)}, u32[]{:S(2)}) collective-permute-start(f32[128,128]{1,0:T(8,128)S(1)} %bitcast_reduce_fusion.ours_ref), channel_id=1, source_target_pairs={{0,8},{8,0},{16,24},{24,16},{32,40},{40,32},{48,56},{56,48},{64,72... | collective-permute-start | bytes 196616 | tf_op jit(solution)/shard_map/ppermute | solution.py:270
  115.0 5.8 %copy-start.1 = (bf16[16,2048,256]{2,1,0:T(8,128)(2,1)S(1)}, bf16[16,2048,256]{2,1,0:T(8,128)(2,1)}, u32[]{:S(2)}) copy-start(bf16[16,2048,256]{2,1,0:T(8,128)(2,1)} %copy-done) | copy-start | bytes 50331652
  138.0 14.3 %all-to-all-start.5 = ((f32[128,1,256]{2,1,0:T(1,128)}), f32[128,1,256]{2,1,0:T(1,128)S(1)}, u32[]{:S(2)}, u32[]{:S(2)}) async-start(f32[128,1,256]{2,1,0:T(1,128)} %broadcast_in_dim.5), calls=%async_computation.5 | async-start | bytes 262144 | tf_op jit(solution)/shard_map/all_to_all | solution.py:283

commit v2 on v1

--- a/solution.py
+++ b/solution.py
@@ -5,15 +5,17 @@
 from jax.experimental.pallas import tpu as pltpu
 from jax.sharding import PartitionSpec as P
 
+LIM1 = 12
 f32 = jnp.float32
 bf16 = jnp.bfloat16
 highest = lax.Precision.HIGHEST
 WHOLE = pl.BlockSpec(memory_space=pltpu.VMEM)
 MIB = 1 << 20
 AHEAD = 3
-
-
-def call(kernel, outs, name, in_specs, limit=12, scratch=()):
+PAD = 8
+
+
+def call(kernel, outs, name, in_specs, limit=4, scratch=()):
     return pl.pallas_call(
         kernel,
         in_specs=in_specs,
@@ -87,11 +89,16 @@
     return approx * left * right
 
 
-def neuron_pass(spikes_hbm, time_ref, trial_ref, spikes_ref, projected_ref, part_ref, sems):
-    trials = spikes_ref.shape[0]
+def neuron_pass(spikes_hbm, time_hbm, trial_hbm, spikes_ref, projected_ref, part_ref, time_ref, trial_ref, sems):
+    trials = projected_ref.shape[0]
     blocks, extended, _ = part_ref.shape
     rows = extended - trials
-    trial = trial_ref[...].astype(f32)
+    small = [
+        pltpu.make_async_copy(time_hbm, time_ref, sems.at[blocks]),
+        pltpu.make_async_copy(trial_hbm, trial_ref, sems.at[blocks + 1]),
+    ]
+    for copy in small:
+        copy.start()
     copies = []
     for b in range(blocks):
         span = pl.ds(b * rows, rows)
@@ -100,6 +107,9 @@
         )
     for b in range(min(AHEAD, blocks)):
         copies[b].start()
+    for copy in small:
+        copy.wait()
+    trial = trial_ref[...].astype(f32)
     for b in range(blocks):
         copies[b].wait()
         if b + AHEAD < blocks:
@@ -115,7 +125,7 @@
         part_ref[b, rows:extended, :] = trial
 
 
-def sum_blocks(parts_ref, copies_ref, trial_ref):
+def neuron_solve(parts_ref, time_ref, held_ref, kept_ref, copies_ref, gram_time_ref, trial_ref, *work):
     blocks, rows, _ = copies_ref.shape
     extended = parts_ref.shape[1]
     trials = extended - rows
@@ -123,32 +133,54 @@
     for b in range(1, blocks):
         total = total + parts_ref[b, 0:rows, :]
     for b in range(blocks):
-        copies_ref[b] = total
-        trial_ref[b * trials : (b + 1) * trials, :] = parts_ref[b, rows:extended, :]
-
-
-def first_system(time_ref, trial_ref, inverse_ref, gram_time_ref, *work):
+        trial_ref[b * trials : (b + 1) * trials, :] = parts_ref[b, rows:extended, :].astype(bf16)
     across = (((0,), (0,)), ((), ()))
-    trial = trial_ref[...].astype(bf16)
     gram_time = lax.dot_general(time_ref[...], time_ref[...], across, preferred_element_type=f32)
-    gram_trial = lax.dot_general(trial, trial, across, preferred_element_type=f32)
+    gram_trial = lax.dot_general(trial_ref[...], trial_ref[...], across, preferred_element_type=f32)
     gram_time_ref[...] = gram_time
-    inverse_ref[...] = inverse(gram_time * gram_trial, *work)
-
-
-def neuron_solve(mttkrp_ref, inverse_ref, raw_ref, gram_ref):
-    raw = dot(mttkrp_ref[...], inverse_ref[...])
-    raw_ref[...] = raw
-    gram_ref[...] = dot(raw, raw, ((0,), (0,)))
-
-
-def trial_pass(count, grams_ref, raw_ref, projected_ref, new_ref, flipped_ref, gram_ref, part_ref, half_ref):
+    raw = dot(total, inverse(gram_time * gram_trial, *work))
+    for b in range(blocks):
+        copies_ref[b] = raw
+
+
+def pack_gram(ours_ref, theirs_ref, packed_ref):
+    blocks, extended, components = packed_ref.shape
+    rows = components // blocks
+    gram = ours_ref[...] + theirs_ref[...]
+    diagonal = jnp.sum(gram * identity(components), axis=0, keepdims=True)
+    for d in range(blocks):
+        packed_ref[d, 0:rows, :] = gram[d * rows : (d + 1) * rows, :]
+        packed_ref[d, rows:extended, :] = jnp.broadcast_to(diagonal, (extended - rows, components))
+
+
+def neuron_gram(raw_ref, held_ref, kept_ref, gram_ref):
+    components = raw_ref.shape[1]
+    raw = raw_ref[...]
+    upper = raw.astype(bf16)
+    lower = (raw - upper.astype(f32)).astype(bf16)
+    split = jnp.concatenate([upper, lower], axis=1)
+    full = lax.dot_general(split, split, (((0,), (0,)), ((), ())), preferred_element_type=f32)
+    gram_ref[...] = (
+        full[:components, :components]
+        + (full[:components, components:] + full[components:, :components])
+        + full[components:, components:]
+    )
+
+
+def trial_pass(count, grams_ref, raw_ref, projected_ref, kept_ref, new_ref, flipped_ref, part_ref, half_ref):
     trials, rows, components = projected_ref.shape
-    gram_raw = jnp.sum(grams_ref[...], axis=0)
-    diagonal = gram_raw * identity(components)
-    scale = jnp.sqrt(jnp.sum(diagonal, axis=0, keepdims=True) / count + 1e-06)
-    scale_down = jnp.sqrt(jnp.sum(diagonal, axis=1, keepdims=True) / count + 1e-06)
-    gram_ref[...] = gram_raw / (scale * scale_down)
+    tri = lax.axis_size("tri")
+    gram = jnp.sum(grams_ref[...], axis=0)
+    lines = components // grams_ref.shape[0]
+    scale = jnp.sqrt(gram[lines : lines + 1, :] / count + 1e-06)
+    share = lines // tri
+    first = lax.axis_index("tri") * share
+    place = lax.broadcasted_iota(jnp.int32, (lines, components), 0)
+    spot = lax.broadcasted_iota(jnp.int32, (PAD, components), 0)
+    sent = jnp.zeros((PAD, components), f32)
+    for i in range(share):
+        line = jnp.sum(jnp.where(place == first + i, gram[0:lines, :], 0.0), axis=0, keepdims=True)
+        sent = jnp.where(spot == i, line, sent)
     new = raw_ref[...] / scale
     new_ref[...] = new
     flipped_ref[...] = new.T
@@ -167,15 +199,39 @@
     totals = lax.fori_loop(0, rows // block, step, [jnp.zeros((8, components), f32)] * trials)
     part = jnp.concatenate([jnp.sum(total, axis=0, keepdims=True) for total in totals], axis=0)
     for d in range(part_ref.shape[0]):
-        part_ref[d] = part
-
-
-def second_system(gram_time_ref, gram_ref, inverse_ref, *work):
-    inverse_ref[...] = inverse(gram_time_ref[...] * gram_ref[...], *work)
+        part_ref[d, 0:trials, :] = part
+        part_ref[d, trials:, :] = sent
+
+
+def trial_sum(gathered_ref, kept_ref, sum_ref):
+    tri = lax.axis_size("tri")
+    chips = gathered_ref.shape[0]
+    trials = gathered_ref.shape[1] - PAD
+    for t in range(tri):
+        total = gathered_ref[t, 0:trials, :]
+        for d in range(t + tri, chips, tri):
+            total = total + gathered_ref[d, 0:trials, :]
+        sum_ref[t * trials : (t + 1) * trials, :] = total
+
+
+def second_system(count, gram_time_ref, gathered_ref, kept_ref, inverse_ref, gram_ref, *work):
+    components = gram_ref.shape[0]
+    chips = gathered_ref.shape[0]
+    trials = gathered_ref.shape[1] - PAD
+    share = components // chips
+    for d in range(chips):
+        gram_ref[d * share : (d + 1) * share, :] = gathered_ref[d, trials : trials + share, :]
+    gram_raw = gram_ref[...]
+    diagonal = gram_raw * identity(components)
+    scale = jnp.sqrt(jnp.sum(diagonal, axis=0, keepdims=True) / count + 1e-06)
+    scale_down = jnp.sqrt(jnp.sum(diagonal, axis=1, keepdims=True) / count + 1e-06)
+    gram = gram_raw / (scale * scale_down)
+    gram_ref[...] = gram
+    inverse_ref[...] = inverse(gram_time_ref[...] * gram, *work)
 
 
 def time_pass(
-    here_ref, ours_ref, theirs_ref, inverse_ref, gram_neuron_ref, flipped_ref, spikes_ref,
+    ours_ref, theirs_ref, inverse_ref, gram_neuron_ref, flipped_ref, spikes_ref,
     trial_ref, system_ref, part_ref, table_ref,
 ):
     trials, rows, bins = spikes_ref.shape
@@ -188,7 +244,7 @@
     scale_down = jnp.sqrt(jnp.sum(diagonal, axis=1, keepdims=True) / count + 1e-06)
     system_ref[...] = gram_neuron_ref[...] * (gram_raw / (scale * scale_down))
     table_ref[...] = raw / scale
-    own = table_ref[pl.ds(pl.multiple_of(here_ref[0] * trials, trials), trials), :]
+    own = table_ref[pl.ds(pl.multiple_of(lax.axis_index("tri") * trials, trials), trials), :]
     trial_ref[...] = own
     columns = own.T
     total = None
@@ -218,7 +274,10 @@
     half = neu // 2
     both = ("neu", "tri")
     swap = [(i, i ^ 1) for i in range(neu)]
-    any_memory = pl.BlockSpec(memory_space=pl.ANY)
+    in_hbm = pl.BlockSpec(memory_space=pltpu.HBM)
+
+    square = array(components, components)
+    work = [pltpu.VMEM((components, components), f32)] * 3
 
     spikes, projected, part = call(
         neuron_pass,
@@ -228,57 +287,59 @@
             array(tri, block + trials, components),
         ],
         "neuron_pass",
-        [any_memory, WHOLE, WHOLE],
-        16,
-        [pltpu.SemaphoreType.DMA((tri,))],
+        [in_hbm] * 3,
+        LIM1,
+        [
+            pltpu.VMEM(time_factor.shape, bf16),
+            pltpu.VMEM((trials, components), bf16),
+            pltpu.SemaphoreType.DMA((tri + 2,)),
+        ],
     )(spike_counts, time_factor, trial_factor)
     parts = lax.all_to_all(part, "tri", 0, 0)
-    copies, trial_old = call(
-        sum_blocks, [array(tri, block, components), array(tri * trials, components)], "sum_blocks", [WHOLE]
-    )(parts)
-    mttkrp_neuron = lax.all_to_all(copies, "tri", 0, 0).reshape(rows, components)
-    square = array(components, components)
-    work = [pltpu.VMEM((components, components), f32)] * 3
-    inverse_one, gram_time = call(first_system, [square, square], "first_system", [WHOLE] * 2, 12, work)(
-        time_factor, trial_old
-    )
-    raw, gram_part = call(neuron_solve, [array(rows, components), square], "neuron_solve", [WHOLE] * 2)(
-        mttkrp_neuron, inverse_one
-    )
-    gram_part = gram_part + lax.ppermute(gram_part, "neu", swap)
+    copies, gram_time = call(
+        neuron_solve,
+        [array(tri, block, components), square],
+        "neuron_solve",
+        [WHOLE] * 4,
+        5,
+        [pltpu.VMEM((tri * trials, components), bf16)] + work,
+    )(parts, time_factor, projected, spikes)
+    raw = lax.all_to_all(copies, "tri", 0, 0).reshape(rows, components)
+    (gram_part,) = call(neuron_gram, [square], "neuron_gram", [WHOLE] * 3)(raw, projected, spikes)
+    (packed,) = call(
+        pack_gram, [array(half, components // half + PAD, components)], "pack_gram", [WHOLE] * 2
+    )(gram_part, lax.ppermute(gram_part, "neu", swap))
     groups = [list(range(c, neu, 2)) for c in range(2)]
-    grams = lax.all_to_all(
-        jnp.broadcast_to(gram_part[None], (half, components, components)), "neu", 0, 0, axis_index_groups=groups
-    )
-    neuron_new, flipped, gram_neuron, trial_part = call(
+    grams = lax.all_to_all(packed, "neu", 0, 0, axis_index_groups=groups)
+    neuron_new, flipped, trial_part = call(
         lambda *refs: trial_pass(neu * rows, *refs),
         [
             array(rows, components),
             array(components, rows),
-            square,
-            array(half * tri, trials, components),
+            array(half * tri, trials + PAD, components),
         ],
         "trial_pass",
-        [WHOLE] * 3,
-        12,
+        [WHOLE] * 4,
+        5,
         [pltpu.VMEM((rows, components), f32)],
-    )(grams, raw, projected)
+    )(grams, raw, projected, spikes)
     groups = [[n * tri + t for n in range(c, neu, 2) for t in range(tri)] for c in range(2)]
     gathered = lax.all_to_all(trial_part, both, 0, 0, axis_index_groups=groups)
-    (inverse_two,) = call(second_system, [square], "second_system", [WHOLE] * 2, 12, work)(gram_time, gram_neuron)
-    ours = jnp.sum(gathered.reshape(half, tri * trials, components), axis=0)
+    (ours,) = call(trial_sum, [array(tri * trials, components)], "trial_sum", [WHOLE] * 2)(gathered, spikes)
     theirs = lax.ppermute(ours, "neu", swap)
-    here = lax.axis_index("tri").astype(jnp.int32).reshape(1)
+    inverse_two, gram_neuron = call(
+        lambda *refs: second_system(neu * rows, *refs), [square, square], "second_system", [WHOLE] * 3, 4, work
+    )(gram_time, gathered, spikes)
     trial_new, system_three, time_part = call(
         time_pass,
         [array(trials, components), square, array(components, bins)],
         "time_pass",
-        [pl.BlockSpec(memory_space=pltpu.SMEM)] + [WHOLE] * 6,
-        12,
+        [WHOLE] * 6,
+        5,
         [pltpu.VMEM((tri * trials, components), f32)],
-    )(here, ours, theirs, inverse_two, gram_neuron, flipped, spikes)
+    )(ours, theirs, inverse_two, gram_neuron, flipped, spikes)
     pieces = lax.all_to_all(time_part.reshape(neu * tri, components // (neu * tri), bins), both, 0, 0)
-    (inverse_three,) = call(third_system, [square], "third_system", [WHOLE], 12, work)(system_three)
+    (inverse_three,) = call(third_system, [square], "third_system", [WHOLE], 4, work)(system_three)
     piece = jnp.sum(pieces, axis=0, keepdims=True)
     mttkrp_time = lax.all_to_all(jnp.broadcast_to(piece, pieces.shape), both, 0, 0).reshape(components, bins)
     time_new, weights = call(time_solve, [array(bins, components), array(1, components)], "time_solve", [WHOLE] * 2)(

time: 154 us -> 128 us (0.83)
  local copies, waits for them, and re-layouts: 25.4 us -> 2.39 us
  blocking collectives: 68.7 us -> 81.2 us
  waiting for transfers between devices: 16 us -> 7.16 us
  starting transfers between devices: 15 us -> 11.3 us
  Pallas kernels: 27.3 us -> 24.6 us
    unnamed x15 -> x5, local copies, waits for them, and re-layouts: 24.5 us -> 1.53 us
    all_to_all x1 -> x2, blocking collectives: 16.2 us -> 28.5 us  [the longest x1 15.5 us: body(): raw = lax.all_to_all(copies, 'tri', 0, 0).reshape(rows, components)]
    all_to_all x1 -> x0, waiting for transfers between devices: 8.85 us -> none  [body(): lax.all_to_all(copies, 'tri', 0, 0).reshape(rows, components)]
    all_to_all x1 -> x0, starting transfers between devices: 3.56 us -> none  [body(): lax.all_to_all(copies, 'tri', 0, 0).reshape(rows, components)]
    pallas_call x5 -> x6, Pallas kernels: 13.2 us -> 10.2 us  [the longest x1 3.82 us: body(): call(third_system, [square], 'third_system', [WHOLE], 4, work)(system_three)]
  transfers between devices with their start and end apart: 4 -> 3, of which waited for: 3 -> 2; matrix products, arithmetic and copies ran while one was open for 0% -> 0% of each run, Pallas kernels for 6% -> 5%
where the time goes in v2:
time: 128 us; the launch traced here: 127 us
  blocking collectives  81.2 us (63%)
  Pallas kernels  24.6 us (19%)
  starting transfers between devices  11.3 us (9%)
  waiting for transfers between devices  7.16 us (6%)
  local copies, waits for them, and re-layouts  2.39 us (2%)
    all_to_all x1, blocking collectives, body(): parts = lax.all_to_all(part, 'tri', 0, 0)  21.9 us
    all_to_all x1, blocking collectives, body(): gathered = lax.all_to_all(trial_part, both, 0, 0, axis_index_groups=groups)  17.8 us
    all_to_all x1, blocking collectives, body(): raw = lax.all_to_all(copies, 'tri', 0, 0).reshape(rows, components)  15.5 us
    all_to_all x1, blocking collectives, body(): lax.all_to_all(time_part.reshape(neu * tri, components // (neu * tri), bi...  13 us
    all_to_all x1, blocking collectives, body(): grams = lax.all_to_all(packed, 'neu', 0, 0, axis_index_groups=groups)  12.9 us
    pallas_call x1, Pallas kernels, body(): call(neuron_pass, [pltpu.VMEM(spike_counts.shape, bf16), pltpu.VMEM((tria...  7.33 us
    all_to_all x1, waiting for transfers between devices, body(): lax.all_to_all(jnp.broadcast_to(piece, pieces.shape), both, 0, 0)  6.25 us
    all_to_all x1, starting transfers between devices, body(): lax.all_to_all(jnp.broadcast_to(piece, pieces.shape), both, 0, 0)  4.26 us
  transfers between devices with their start and end apart: 3, of which 2 were waited for; matrix products, arithmetic and copies ran while one was open for 0% of the time, Pallas kernels for 5%

profile of v2, /device:TPU:1, one launch (start us, length us, event | category | flops | bytes accessed | tf_op | source)
XLA Modules:
  0.0 127.5 jit_solution(5186427386023055297)
XLA Ops:
  0.6 0.0 copy-start
  0.6 0.8 copy-done
  1.5 0.0 copy-start.1
  1.5 0.7 copy-done.1
  2.2 7.3 %neuron_pass.1 = (bf16[16,2048,256]{2,1,0:T(8,128)(2,1)S(1)}, f32[16,2048,128]{2,1,0:T(8,128)S(1)}, f32[8,272,128]{2,1,0:T(8,128)S(1)}) custom-call(bf16[16,2048,256]{2,1,0:T(8,128)(2,1)} %spikes_hbm.1, bf16[256,128]{1,0:T(8,128)(2,1)S(1)} %copy-done, bf16[16,128]{1,0:T(8,128)(2,1)S(1)} %copy-done.1), custom_call_target="tpu_custom_call" | custom-call | tf_op jit(solution)/shard_map/neuron_pass/pallas_call | solution.py:282
  9.5 21.9 %all_to_all.30.parts_ref = f32[8,272,128]{2,1,0:T(8,128)S(1)} all-to-all(f32[8,272,128]{2,1,0:T(8,128)S(1)} %get-tuple-element.19), channel_id=1, replica_groups=mesh['neu'=16,'tri'=8] {'tri'}, dimensions={0} | all-to-all | bytes 2228224 | tf_op jit(solution)/shard_map/all_to_all | solution.py:298
  31.4 3.2 %neuron_solve.1 = (f32[8,256,128]{2,1,0:T(8,128)S(1)}, f32[128,128]{1,0:T(8,128)S(1)}) custom-call(f32[8,272,128]{2,1,0:T(8,128)S(1)} %all_to_all.30.parts_ref, bf16[256,128]{1,0:T(8,128)(2,1)S(1)} %copy-done, f32[16,2048,128]{2,1,0:T(8,128)S(1)} %get-tuple-element.20.held_ref.refs_2_, ...), custom_call_target="tpu_custom_call" | custom-call | tf_op jit(solution)/shard_map/neuron_solve/pallas_call | solution.py:299
  34.6 15.5 %all_to_all.31 = f32[8,256,128]{2,1,0:T(8,128)S(1)} all-to-all(f32[8,256,128]{2,1,0:T(8,128)S(1)} %get-tuple-element.22), channel_id=1, replica_groups=mesh['neu'=16,'tri'=8] {'tri'}, dimensions={0} | all-to-all | bytes 2097152 | tf_op jit(solution)/shard_map/all_to_all | solution.py:307
  50.1 0.5 neuron_gram.1.ours_ref
  50.6 3.8 %collective-permute-start = (f32[128,128]{1,0:T(8,128)S(1)}, f32[128,128]{1,0:T(8,128)S(1)}, u32[]{:S(2)}, u32[]{:S(2)}) collective-permute-start(f32[128,128]{1,0:T(8,128)S(1)} %neuron_gram.1.ours_ref), channel_id=1, source_target_pairs={{0,8},{8,0},{16,24},{24,16},{32,40},{40,32},{48,56},{56,48},{64,72... | collective-permute-start | bytes 196616 | tf_op jit(solution)/shard_map/ppermute | solution.py:311
  54.4 0.9 collective-permute-done.theirs_ref
  55.3 12.9 %all_to_all.32.refs_0_ = f32[8,24,128]{2,1,0:T(8,128)S(1)} all-to-all(f32[8,24,128]{2,1,0:T(8,128)S(1)} %pack_gram.1), channel_id=1, replica_groups={{0,16,32,48,64,80,96,112},{8,24,40,56,72,88,104,120},{1,17,33,49,65,81,..., dimensions={0} | all-to-all | bytes 196608 | tf_op jit(solution)/shard_map/all_to_all | solution.py:313
  68.3 2.7 %trial_pass.1 = (f32[2048,128]{1,0:T(8,128)}, f32[128,2048]{1,0:T(8,128)S(1)}, f32[64,24,128]{2,1,0:T(8,128)S(1)}) custom-call(f32[8,24,128]{2,1,0:T(8,128)S(1)} %all_to_all.32.refs_0_, f32[2048,128]{1,0:T(8,128)S(1)} %bitcast.7, f32[16,2048,128]{2,1,0:T(8,128)S(1)} %get-tuple-element.20.held_ref.refs_2_, ...), custom_call_target="tpu_custom_call" | custom-call | tf_op jit(solution)/shard_map/trial_pass/pallas_call | solution.py:314
  71.0 17.8 %all_to_all.33.gathered_ref.refs_1_ = f32[64,24,128]{2,1,0:T(8,128)S(1)} all-to-all(f32[64,24,128]{2,1,0:T(8,128)S(1)} %get-tuple-element.24), channel_id=1, replica_groups={{0,1,2,3,4,5,6,7,16,17,18,19,20,21,22,23,32,33,34,35,36,37,38,39,48,49,..., dimensions={0} | all-to-all | bytes 1572864 | tf_op jit(solution)/shard_map/all_to_all | solution.py:327
  88.9 3.2 %collective-permute-start.1 = (f32[128,128]{1,0:T(8,128)S(1)}, f32[128,128]{1,0:T(8,128)S(1)}, u32[]{:S(2)}, u32[]{:S(2)}) collective-permute-start(f32[128,128]{1,0:T(8,128)S(1)} %trial_sum.1.ours_ref), channel_id=1, source_target_pairs={{0,8},{8,0},{16,24},{24,16},{32,40},{40,32},{48,56},{56,48},{64,72... | collective-permute-start | bytes 196616 | tf_op jit(solution)/shard_map/ppermute | solution.py:329
  92.1 2.6 %second_system.1 = (f32[128,128]{1,0:T(8,128)S(1)}, f32[128,128]{1,0:T(8,128)S(1)}) custom-call(f32[128,128]{1,0:T(8,128)S(1)} %get-tuple-element.25.refs_0_, f32[64,24,128]{2,1,0:T(8,128)S(1)} %all_to_all.33.gathered_ref.refs_1_, bf16[16,2048,256]{2,1,0:T(8,128)(2,1)S(1)} %get-tuple-element.21.kept_ref.refs_3_.refs_2_.spikes_ref), custom_call_target="tpu_custom_call" | custom-call | tf_op jit(solution)/shard_map/second_system/pallas_call | solution.py:330
  94.7 0.0 collective-permute-done.1.theirs_ref
  94.7 3.3 %time_pass.1 = (f32[16,128]{1,0:T(8,128)}, f32[128,128]{1,0:T(8,128)S(1)}, f32[128,256]{1,0:T(8,128)S(1)}) custom-call(f32[128,128]{1,0:T(8,128)S(1)} %trial_sum.1.ours_ref, f32[128,128]{1,0:T(8,128)S(1)} %collective-permute-done.1.theirs_ref, f32[128,128]{1,0:T(8,128)S(1)} %get-tuple-element.26.inverse_ref, ...), custom_call_target="tpu_custom_call" | custom-call | tf_op jit(solution)/shard_map/time_pass/pallas_call | solution.py:333
  98.0 0.1 copy.7
  98.1 13.0 %all_to_all.34 = f32[128,1,256]{2,1,0:T(1,128)S(1)} all-to-all(f32[128,1,256]{2,1,0:T(1,128)S(1)} %copy.7), channel_id=1, replica_groups=mesh['neu'=16,'tri'=8] {'neu','tri'}, dimensions={0} | all-to-all | bytes 262144 | tf_op jit(solution)/shard_map/all_to_all | solution.py:341
  111.2 0.2 reduce_sum.9
  111.3 0.7 broadcast_in_dim.2
  112.1 4.3 %all-to-all-start.5 = ((f32[128,1,256]{2,1,0:T(1,128)}), f32[128,1,256]{2,1,0:T(1,128)S(1)}, u32[]{:S(2)}, u32[]{:S(2)}) async-start(f32[128,1,256]{2,1,0:T(1,128)} %broadcast_in_dim.2), calls=%async_computation.5 | async-start | bytes 262144 | tf_op jit(solution)/shard_map/all_to_all | solution.py:344
  116.3 3.8 %third_system.1.inverse_ref = f32[128,128]{1,0:T(8,128)S(1)} custom-call(f32[128,128]{1,0:T(8,128)S(1)} %get-tuple-element.31.system_ref), custom_call_target="tpu_custom_call" | custom-call | tf_op jit(solution)/shard_map/third_system/pallas_call | solution.py:342
  120.2 6.3 %all-to-all-done.5 = f32[128,1,256]{2,1,0:T(1,128)S(1)} async-done(((f32[128,1,256]{2,1,0:T(1,128)}), f32[128,1,256]{2,1,0:T(1,128)S(1)}, u32[]{:S(2)}, u32[]{:S(2)}) %all-to-all-start.5) | async-done | bytes 131104 | tf_op jit(solution)/shard_map/all_to_all | solution.py:344
  126.4 1.0 time_solve.1
  (3 shorter events, 0.1 us)
Async XLA Ops:
  0.6 0.8 copy-start
  1.5 0.7 copy-start.1
  50.6 4.7 %collective-permute-start = (f32[128,128]{1,0:T(8,128)S(1)}, f32[128,128]{1,0:T(8,128)S(1)}, u32[]{:S(2)}, u32[]{:S(2)}) collective-permute-start(f32[128,128]{1,0:T(8,128)S(1)} %neuron_gram.1.ours_ref), channel_id=1, source_target_pairs={{0,8},{8,0},{16,24},{24,16},{32,40},{40,32},{48,56},{56,48},{64,72... | collective-permute-start | bytes 196616 | tf_op jit(solution)/shard_map/ppermute | solution.py:311
  88.9 5.8 %collective-permute-start.1 = (f32[128,128]{1,0:T(8,128)S(1)}, f32[128,128]{1,0:T(8,128)S(1)}, u32[]{:S(2)}, u32[]{:S(2)}) collective-permute-start(f32[128,128]{1,0:T(8,128)S(1)} %trial_sum.1.ours_ref), channel_id=1, source_target_pairs={{0,8},{8,0},{16,24},{24,16},{32,40},{40,32},{48,56},{56,48},{64,72... | collective-permute-start | bytes 196616 | tf_op jit(solution)/shard_map/ppermute | solution.py:329
  112.1 14.3 %all-to-all-start.5 = ((f32[128,1,256]{2,1,0:T(1,128)}), f32[128,1,256]{2,1,0:T(1,128)S(1)}, u32[]{:S(2)}, u32[]{:S(2)}) async-start(f32[128,1,256]{2,1,0:T(1,128)} %broadcast_in_dim.2), calls=%async_computation.5 | async-start | bytes 262144 | tf_op jit(solution)/shard_map/all_to_all | solution.py:344

commit v3 on v2

--- a/solution.py
+++ b/solution.py
@@ -15,16 +15,20 @@
 PAD = 8
 
 
-def call(kernel, outs, name, in_specs, limit=4, scratch=()):
+def call(kernel, outs, name, in_specs, limit=4, scratch=(), out_specs=None):
     return pl.pallas_call(
         kernel,
         in_specs=in_specs,
-        out_specs=[WHOLE] * len(outs),
+        out_specs=out_specs or [WHOLE] * len(outs),
         out_shape=outs,
         scratch_shapes=scratch,
         compiler_params=pltpu.CompilerParams(vmem_limit_bytes=limit * MIB),
         name=name,
     )
+
+
+def held(value):
+    return pltpu.with_memory_space_constraint(value, pltpu.VMEM)
 
 
 def array(*shape):
@@ -181,7 +185,7 @@
     for i in range(share):
         line = jnp.sum(jnp.where(place == first + i, gram[0:lines, :], 0.0), axis=0, keepdims=True)
         sent = jnp.where(spot == i, line, sent)
-    new = raw_ref[...] / scale
+    new = raw_ref[...] * (1.0 / scale)
     new_ref[...] = new
     flipped_ref[...] = new.T
     half_ref[...] = new.astype(bf16).astype(f32)
@@ -196,7 +200,7 @@
             for k in range(trials)
         ]
 
-    totals = lax.fori_loop(0, rows // block, step, [jnp.zeros((8, components), f32)] * trials)
+    totals = lax.fori_loop(0, rows // block, step, [jnp.zeros((8, components), f32)] * trials, unroll=2)
     part = jnp.concatenate([jnp.sum(total, axis=0, keepdims=True) for total in totals], axis=0)
     for d in range(part_ref.shape[0]):
         part_ref[d, 0:trials, :] = part
@@ -231,9 +235,11 @@
 
 
 def time_pass(
-    ours_ref, theirs_ref, inverse_ref, gram_neuron_ref, flipped_ref, spikes_ref,
-    trial_ref, system_ref, part_ref, table_ref,
+    ours_ref, theirs_ref, inverse_ref, gram_neuron_ref, flipped_ref, spikes_ref, new_ref,
+    new_hbm, trial_hbm, system_hbm, part_ref, table_ref, system_ref, sems,
 ):
+    new_copy = pltpu.make_async_copy(new_ref, new_hbm, sems.at[0])
+    new_copy.start()
     trials, rows, bins = spikes_ref.shape
     components = inverse_ref.shape[0]
     raw = dot(ours_ref[...] + theirs_ref[...], inverse_ref[...])
@@ -244,15 +250,22 @@
     scale_down = jnp.sqrt(jnp.sum(diagonal, axis=1, keepdims=True) / count + 1e-06)
     system_ref[...] = gram_neuron_ref[...] * (gram_raw / (scale * scale_down))
     table_ref[...] = raw / scale
-    own = table_ref[pl.ds(pl.multiple_of(lax.axis_index("tri") * trials, trials), trials), :]
-    trial_ref[...] = own
-    columns = own.T
+    span = pl.ds(pl.multiple_of(lax.axis_index("tri") * trials, trials), trials)
+    copies = [
+        pltpu.make_async_copy(table_ref.at[span, :], trial_hbm, sems.at[1]),
+        pltpu.make_async_copy(system_ref, system_hbm, sems.at[2]),
+    ]
+    for copy in copies:
+        copy.start()
+    columns = table_ref[span, :].T
     total = None
     for k in range(trials):
         khatri_rao = (flipped_ref[...] * columns[:, k : k + 1]).astype(bf16)
         term = jnp.dot(khatri_rao, spikes_ref[k], preferred_element_type=f32)
         total = term if total is None else total + term
     part_ref[...] = total
+    for copy in [new_copy] + copies:
+        copy.wait()
 
 
 def third_system(system_ref, inverse_ref, *work):
@@ -294,7 +307,7 @@
             pltpu.VMEM((trials, components), bf16),
             pltpu.SemaphoreType.DMA((tri + 2,)),
         ],
-    )(spike_counts, time_factor, trial_factor)
+    )(spike_counts, *[pltpu.with_memory_space_constraint(a, pltpu.HBM) for a in (time_factor, trial_factor)])
     parts = lax.all_to_all(part, "tri", 0, 0)
     copies, gram_time = call(
         neuron_solve,
@@ -303,15 +316,15 @@
         [WHOLE] * 4,
         5,
         [pltpu.VMEM((tri * trials, components), bf16)] + work,
-    )(parts, time_factor, projected, spikes)
+    )(parts, time_factor, held(projected), held(spikes))
     raw = lax.all_to_all(copies, "tri", 0, 0).reshape(rows, components)
-    (gram_part,) = call(neuron_gram, [square], "neuron_gram", [WHOLE] * 3)(raw, projected, spikes)
+    (gram_part,) = call(neuron_gram, [square], "neuron_gram", [WHOLE] * 3)(raw, held(projected), held(spikes))
     (packed,) = call(
         pack_gram, [array(half, components // half + PAD, components)], "pack_gram", [WHOLE] * 2
     )(gram_part, lax.ppermute(gram_part, "neu", swap))
     groups = [list(range(c, neu, 2)) for c in range(2)]
     grams = lax.all_to_all(packed, "neu", 0, 0, axis_index_groups=groups)
-    neuron_new, flipped, trial_part = call(
+    new, flipped, trial_part = call(
         lambda *refs: trial_pass(neu * rows, *refs),
         [
             array(rows, components),
@@ -322,22 +335,27 @@
         [WHOLE] * 4,
         5,
         [pltpu.VMEM((rows, components), f32)],
-    )(grams, raw, projected, spikes)
+    )(grams, raw, held(projected), held(spikes))
     groups = [[n * tri + t for n in range(c, neu, 2) for t in range(tri)] for c in range(2)]
     gathered = lax.all_to_all(trial_part, both, 0, 0, axis_index_groups=groups)
-    (ours,) = call(trial_sum, [array(tri * trials, components)], "trial_sum", [WHOLE] * 2)(gathered, spikes)
+    (ours,) = call(trial_sum, [array(tri * trials, components)], "trial_sum", [WHOLE] * 2)(gathered, held(spikes))
     theirs = lax.ppermute(ours, "neu", swap)
     inverse_two, gram_neuron = call(
         lambda *refs: second_system(neu * rows, *refs), [square, square], "second_system", [WHOLE] * 3, 4, work
-    )(gram_time, gathered, spikes)
-    trial_new, system_three, time_part = call(
+    )(gram_time, gathered, held(spikes))
+    neuron_new, trial_new, system_three, time_part = call(
         time_pass,
-        [array(trials, components), square, array(components, bins)],
+        [array(rows, components), array(trials, components), square, array(components, bins)],
         "time_pass",
-        [WHOLE] * 6,
+        [WHOLE] * 7,
         5,
-        [pltpu.VMEM((tri * trials, components), f32)],
-    )(ours, theirs, inverse_two, gram_neuron, flipped, spikes)
+        [
+            pltpu.VMEM((tri * trials, components), f32),
+            pltpu.VMEM((components, components), f32),
+            pltpu.SemaphoreType.DMA((3,)),
+        ],
+        [in_hbm] * 3 + [WHOLE],
+    )(ours, theirs, inverse_two, gram_neuron, flipped, held(spikes), held(new))
     pieces = lax.all_to_all(time_part.reshape(neu * tri, components // (neu * tri), bins), both, 0, 0)
     (inverse_three,) = call(third_system, [square], "third_system", [WHOLE], 4, work)(system_three)
     piece = jnp.sum(pieces, axis=0, keepdims=True)

time: 128 us -> 125 us (0.977)
  Pallas kernels: 24.6 us -> 22.9 us
  local copies, waits for them, and re-layouts: 2.39 us -> 0.88 us
    unnamed x5 -> x3, local copies, waits for them, and re-layouts: 1.53 us -> 0.01 us
where the time goes in v3:
time: 125 us; the launch traced here: 124 us
  blocking collectives  81.1 us (65%)
  Pallas kernels  22.9 us (18%)
  starting transfers between devices  11.3 us (9%)
  waiting for transfers between devices  7.16 us (6%)
    all_to_all x1, blocking collectives, body(): parts = lax.all_to_all(part, 'tri', 0, 0)  21.9 us
    all_to_all x1, blocking collectives, body(): gathered = lax.all_to_all(trial_part, both, 0, 0, axis_index_groups=groups)  17.8 us
    all_to_all x1, blocking collectives, body(): raw = lax.all_to_all(copies, 'tri', 0, 0).reshape(rows, components)  15.5 us
    all_to_all x1, blocking collectives, body(): lax.all_to_all(time_part.reshape(neu * tri, components // (neu * tri), bi...  13 us
    all_to_all x1, blocking collectives, body(): grams = lax.all_to_all(packed, 'neu', 0, 0, axis_index_groups=groups)  12.8 us
    pallas_call x1, Pallas kernels, body(): call(neuron_pass, [pltpu.VMEM(spike_counts.shape, bf16), pltpu.VMEM((tria...  7.35 us
    all_to_all x1, waiting for transfers between devices, body(): lax.all_to_all(jnp.broadcast_to(piece, pieces.shape), both, 0, 0)  6.25 us
    all_to_all x1, starting transfers between devices, body(): lax.all_to_all(jnp.broadcast_to(piece, pieces.shape), both, 0, 0)  4.26 us
  transfers between devices with their start and end apart: 3, of which 2 were waited for; matrix products, arithmetic and copies ran while one was open for 0% of the time, Pallas kernels for 5%

profile of v3, /device:TPU:1, one launch (start us, length us, event | category | flops | bytes accessed | tf_op | source)
XLA Modules:
  0.0 124.1 jit_solution(4989009697727970089)
XLA Ops:
  0.6 0.0 copy-start
  0.6 7.3 %neuron_pass.1 = (bf16[16,2048,256]{2,1,0:T(8,128)(2,1)S(1)}, f32[16,2048,128]{2,1,0:T(8,128)S(1)}, f32[8,272,128]{2,1,0:T(8,128)S(1)}) custom-call(bf16[16,2048,256]{2,1,0:T(8,128)(2,1)} %spikes_hbm.1, bf16[256,128]{1,0:T(8,128)(2,1)} %time_ref.1, bf16[16,128]{1,0:T(8,128)(2,1)} %trial_hbm.1), custom_call_target="tpu_custom_call" | custom-call | tf_op jit(solution)/shard_map/neuron_pass/pallas_call | solution.py:295
  8.0 21.9 %all_to_all.30.parts_ref = f32[8,272,128]{2,1,0:T(8,128)S(1)} all-to-all(f32[8,272,128]{2,1,0:T(8,128)S(1)} %get-tuple-element.20), channel_id=1, replica_groups=mesh['neu'=16,'tri'=8] {'tri'}, dimensions={0} | all-to-all | bytes 2228224 | tf_op jit(solution)/shard_map/all_to_all | solution.py:311
  29.9 0.0 copy-done
  29.9 2.8 %neuron_solve.1 = (f32[8,256,128]{2,1,0:T(8,128)S(1)}, f32[128,128]{1,0:T(8,128)S(1)}) custom-call(f32[8,272,128]{2,1,0:T(8,128)S(1)} %all_to_all.30.parts_ref, bf16[256,128]{1,0:T(8,128)(2,1)S(1)} %copy-done, f32[16,2048,128]{2,1,0:T(8,128)S(1)} %get-tuple-element.21.held_ref.refs_2_, ...), custom_call_target="tpu_custom_call" | custom-call | tf_op jit(solution)/shard_map/neuron_solve/pallas_call | solution.py:312
  32.6 15.5 %all_to_all.31 = f32[8,256,128]{2,1,0:T(8,128)S(1)} all-to-all(f32[8,256,128]{2,1,0:T(8,128)S(1)} %get-tuple-element.23), channel_id=1, replica_groups=mesh['neu'=16,'tri'=8] {'tri'}, dimensions={0} | all-to-all | bytes 2097152 | tf_op jit(solution)/shard_map/all_to_all | solution.py:320
  48.2 0.5 neuron_gram.1.ours_ref
  48.6 3.8 %collective-permute-start = (f32[128,128]{1,0:T(8,128)S(1)}, f32[128,128]{1,0:T(8,128)S(1)}, u32[]{:S(2)}, u32[]{:S(2)}) collective-permute-start(f32[128,128]{1,0:T(8,128)S(1)} %neuron_gram.1.ours_ref), channel_id=1, source_target_pairs={{0,8},{8,0},{16,24},{24,16},{32,40},{40,32},{48,56},{56,48},{64,72... | collective-permute-start | bytes 196616 | tf_op jit(solution)/shard_map/ppermute | solution.py:324
  52.5 0.9 collective-permute-done.theirs_ref
  53.4 12.8 %all_to_all.32.refs_0_ = f32[8,24,128]{2,1,0:T(8,128)S(1)} all-to-all(f32[8,24,128]{2,1,0:T(8,128)S(1)} %pack_gram.1), channel_id=1, replica_groups={{0,16,32,48,64,80,96,112},{8,24,40,56,72,88,104,120},{1,17,33,49,65,81,..., dimensions={0} | all-to-all | bytes 196608 | tf_op jit(solution)/shard_map/all_to_all | solution.py:326
  66.2 1.6 %trial_pass.1 = (f32[2048,128]{1,0:T(8,128)S(1)}, f32[128,2048]{1,0:T(8,128)S(1)}, f32[64,24,128]{2,1,0:T(8,128)S(1)}) custom-call(f32[8,24,128]{2,1,0:T(8,128)S(1)} %all_to_all.32.refs_0_, f32[2048,128]{1,0:T(8,128)S(1)} %bitcast.7, f32[16,2048,128]{2,1,0:T(8,128)S(1)} %get-tuple-element.21.held_ref.refs_2_, ...), custom_call_target="tpu_custom_call" | custom-call | tf_op jit(solution)/shard_map/trial_pass/pallas_call | solution.py:327
  67.9 17.8 %all_to_all.33.gathered_ref.refs_1_ = f32[64,24,128]{2,1,0:T(8,128)S(1)} all-to-all(f32[64,24,128]{2,1,0:T(8,128)S(1)} %get-tuple-element.24), channel_id=1, replica_groups={{0,1,2,3,4,5,6,7,16,17,18,19,20,21,22,23,32,33,34,35,36,37,38,39,48,49,..., dimensions={0} | all-to-all | bytes 1572864 | tf_op jit(solution)/shard_map/all_to_all | solution.py:340
  85.7 3.2 %collective-permute-start.1 = (f32[128,128]{1,0:T(8,128)S(1)}, f32[128,128]{1,0:T(8,128)S(1)}, u32[]{:S(2)}, u32[]{:S(2)}) collective-permute-start(f32[128,128]{1,0:T(8,128)S(1)} %trial_sum.1.ours_ref), channel_id=1, source_target_pairs={{0,8},{8,0},{16,24},{24,16},{32,40},{40,32},{48,56},{56,48},{64,72... | collective-permute-start | bytes 196616 | tf_op jit(solution)/shard_map/ppermute | solution.py:342
  88.9 2.5 %second_system.1 = (f32[128,128]{1,0:T(8,128)S(1)}, f32[128,128]{1,0:T(8,128)S(1)}) custom-call(f32[128,128]{1,0:T(8,128)S(1)} %get-tuple-element.25.refs_0_, f32[64,24,128]{2,1,0:T(8,128)S(1)} %all_to_all.33.gathered_ref.refs_1_, bf16[16,2048,256]{2,1,0:T(8,128)(2,1)S(1)} %get-tuple-element.22.kept_ref.refs_3_.refs_2_.spikes_ref), custom_call_target="tpu_custom_call" | custom-call | tf_op jit(solution)/shard_map/second_system/pallas_call | solution.py:343
  91.4 0.0 collective-permute-done.1.theirs_ref
  91.5 3.2 %time_pass.1 = (f32[2048,128]{1,0:T(8,128)}, f32[16,128]{1,0:T(8,128)}, f32[128,128]{1,0:T(8,128)S(1)}, f32[128,256]{1,0:T(8,128)S(1)}) custom-call(f32[128,128]{1,0:T(8,128)S(1)} %trial_sum.1.ours_ref, f32[128,128]{1,0:T(8,128)S(1)} %collective-permute-done.1.theirs_ref, f32[128,128]{1,0:T(8,128)S(1)} %get-tuple-element.26.inverse_ref, ...), custom_call_target="tpu_custom_call" | custom-call | tf_op jit(solution)/shard_map/time_pass/pallas_call | solution.py:346
  94.7 0.1 copy.7
  94.8 13.0 %all_to_all.34 = f32[128,1,256]{2,1,0:T(1,128)S(1)} all-to-all(f32[128,1,256]{2,1,0:T(1,128)S(1)} %copy.7), channel_id=1, replica_groups=mesh['neu'=16,'tri'=8] {'neu','tri'}, dimensions={0} | all-to-all | bytes 262144 | tf_op jit(solution)/shard_map/all_to_all | solution.py:359
  107.9 0.2 reduce_sum.9
  108.0 0.7 broadcast_in_dim.2
  108.8 4.3 %all-to-all-start.5 = ((f32[128,1,256]{2,1,0:T(1,128)}), f32[128,1,256]{2,1,0:T(1,128)S(1)}, u32[]{:S(2)}, u32[]{:S(2)}) async-start(f32[128,1,256]{2,1,0:T(1,128)} %broadcast_in_dim.2), calls=%async_computation.5 | async-start | bytes 262144 | tf_op jit(solution)/shard_map/all_to_all | solution.py:362
  113.0 3.8 %third_system.1.inverse_ref = f32[128,128]{1,0:T(8,128)S(1)} custom-call(f32[128,128]{1,0:T(8,128)S(1)} %get-tuple-element.33.system_ref), custom_call_target="tpu_custom_call" | custom-call | tf_op jit(solution)/shard_map/third_system/pallas_call | solution.py:360
  116.8 6.3 %all-to-all-done.5 = f32[128,1,256]{2,1,0:T(1,128)S(1)} async-done(((f32[128,1,256]{2,1,0:T(1,128)}), f32[128,1,256]{2,1,0:T(1,128)S(1)}, u32[]{:S(2)}, u32[]{:S(2)}) %all-to-all-start.5) | async-done | bytes 131104 | tf_op jit(solution)/shard_map/all_to_all | solution.py:362
  123.1 1.0 time_solve.1
  (3 shorter events, 0.1 us)
Async XLA Ops:
  0.6 29.2 %copy-start = (bf16[256,128]{1,0:T(8,128)(2,1)S(1)}, bf16[256,128]{1,0:T(8,128)(2,1)}, u32[]{:S(2)}) copy-start(bf16[256,128]{1,0:T(8,128)(2,1)} %time_ref.1) | copy-start | bytes 196612
  48.6 4.7 %collective-permute-start = (f32[128,128]{1,0:T(8,128)S(1)}, f32[128,128]{1,0:T(8,128)S(1)}, u32[]{:S(2)}, u32[]{:S(2)}) collective-permute-start(f32[128,128]{1,0:T(8,128)S(1)} %neuron_gram.1.ours_ref), channel_id=1, source_target_pairs={{0,8},{8,0},{16,24},{24,16},{32,40},{40,32},{48,56},{56,48},{64,72... | collective-permute-start | bytes 196616 | tf_op jit(solution)/shard_map/ppermute | solution.py:324
  85.7 5.7 %collective-permute-start.1 = (f32[128,128]{1,0:T(8,128)S(1)}, f32[128,128]{1,0:T(8,128)S(1)}, u32[]{:S(2)}, u32[]{:S(2)}) collective-permute-start(f32[128,128]{1,0:T(8,128)S(1)} %trial_sum.1.ours_ref), channel_id=1, source_target_pairs={{0,8},{8,0},{16,24},{24,16},{32,40},{40,32},{48,56},{56,48},{64,72... | collective-permute-start | bytes 196616 | tf_op jit(solution)/shard_map/ppermute | solution.py:342
  108.8 14.3 %all-to-all-start.5 = ((f32[128,1,256]{2,1,0:T(1,128)}), f32[128,1,256]{2,1,0:T(1,128)S(1)}, u32[]{:S(2)}, u32[]{:S(2)}) async-start(f32[128,1,256]{2,1,0:T(1,128)} %broadcast_in_dim.2), calls=%async_computation.5 | async-start | bytes 262144 | tf_op jit(solution)/shard_map/all_to_all | solution.py:362

commit v4 on v3

--- a/solution.py
+++ b/solution.py
@@ -37,6 +37,15 @@
 
 def dot(a, b, dims=((1,), (0,))):
     return lax.dot_general(a, b, (dims, ((), ())), precision=highest, preferred_element_type=f32)
+
+
+def rough(a, b):
+    return jnp.dot(a.astype(bf16), b.astype(bf16), preferred_element_type=f32)
+
+
+def fine(a, b):
+    a_upper, b_upper = a.astype(bf16).astype(f32), b.astype(bf16).astype(f32)
+    return rough(a_upper, b_upper) + (rough(a_upper, b - b_upper) + rough(a - a_upper, b_upper))
 
 
 def identity(n):
@@ -61,31 +70,39 @@
     error = eye - step * scaled
     scaled_ref[...] = scaled
     approx_ref[...] = step * (eye + error)
-    error = dot(error, error)
-    error_ref[...] = error
-
-    def going(state):
-        count, norm = state
-        return (norm > 1e-2) & (count < 40)
-
-    def square(state):
-        error = error_ref[...]
-        approx = approx_ref[...]
-        approx_ref[...] = approx + dot(approx, error)
-        error = dot(error, error)
-        error_ref[...] = error
-        return state[0] + 1, row_norm(error)
-
-    lax.while_loop(going, square, (0, row_norm(error)))
+    near = bound < 1.9
+
+    @pl.when(near)
+    def _():
+        approx_ref[...] = approx_ref[...] + rough(approx_ref[...], rough(error, error))
+
+    @pl.when(jnp.logical_not(near))
+    def _():
+        squared = dot(error, error)
+        error_ref[...] = squared
+
+        def going(state):
+            count, norm = state
+            return (norm > 1e-2) & (count < 40)
+
+        def square(state):
+            error = error_ref[...]
+            approx = approx_ref[...]
+            approx_ref[...] = approx + dot(approx, error)
+            error = dot(error, error)
+            error_ref[...] = error
+            return state[0] + 1, row_norm(error)
+
+        lax.while_loop(going, square, (0, row_norm(squared)))
 
     def refining(state):
         count, norm = state
-        return (norm > 5e-4) & (count < 6)
+        return (norm > 5e-4) & (count < 12)
 
     def refine(state):
         approx = approx_ref[...]
         residual = eye - dot(scaled_ref[...], approx)
-        approx_ref[...] = approx + dot(approx, residual)
+        approx_ref[...] = approx + fine(approx, residual)
         return state[0] + 1, row_norm(residual)
 
     lax.while_loop(refining, refine, (0, jnp.float32(1.0)))
@@ -235,25 +252,20 @@
 
 
 def time_pass(
-    ours_ref, theirs_ref, inverse_ref, gram_neuron_ref, flipped_ref, spikes_ref, new_ref,
-    new_hbm, trial_hbm, system_hbm, part_ref, table_ref, system_ref, sems,
+    ours_ref, theirs_ref, inverse_ref, flipped_ref, spikes_ref, new_ref,
+    new_hbm, trial_hbm, table_hbm, part_ref, table_ref, sems,
 ):
     new_copy = pltpu.make_async_copy(new_ref, new_hbm, sems.at[0])
     new_copy.start()
     trials, rows, bins = spikes_ref.shape
     components = inverse_ref.shape[0]
     raw = dot(ours_ref[...] + theirs_ref[...], inverse_ref[...])
-    gram_raw = dot(raw, raw, ((0,), (0,)))
-    diagonal = gram_raw * identity(components)
-    count = raw.shape[0]
-    scale = jnp.sqrt(jnp.sum(diagonal, axis=0, keepdims=True) / count + 1e-06)
-    scale_down = jnp.sqrt(jnp.sum(diagonal, axis=1, keepdims=True) / count + 1e-06)
-    system_ref[...] = gram_neuron_ref[...] * (gram_raw / (scale * scale_down))
+    scale = jnp.sqrt(jnp.sum(raw * raw, axis=0, keepdims=True) / raw.shape[0] + 1e-06)
     table_ref[...] = raw / scale
     span = pl.ds(pl.multiple_of(lax.axis_index("tri") * trials, trials), trials)
     copies = [
         pltpu.make_async_copy(table_ref.at[span, :], trial_hbm, sems.at[1]),
-        pltpu.make_async_copy(system_ref, system_hbm, sems.at[2]),
+        pltpu.make_async_copy(table_ref, table_hbm, sems.at[2]),
     ]
     for copy in copies:
         copy.start()
@@ -268,8 +280,9 @@
         copy.wait()
 
 
-def third_system(system_ref, inverse_ref, *work):
-    inverse_ref[...] = inverse(system_ref[...], *work)
+def third_system(gram_neuron_ref, table_ref, inverse_ref, *work):
+    table = table_ref[...]
+    inverse_ref[...] = inverse(gram_neuron_ref[...] * dot(table, table, ((0,), (0,))), *work)
 
 
 def time_solve(mttkrp_ref, inverse_ref, time_ref, weights_ref):
@@ -343,21 +356,25 @@
     inverse_two, gram_neuron = call(
         lambda *refs: second_system(neu * rows, *refs), [square, square], "second_system", [WHOLE] * 3, 4, work
     )(gram_time, gathered, held(spikes))
-    neuron_new, trial_new, system_three, time_part = call(
+    neuron_new, trial_new, trial_table, time_part = call(
         time_pass,
-        [array(rows, components), array(trials, components), square, array(components, bins)],
+        [
+            array(rows, components),
+            array(trials, components),
+            array(tri * trials, components),
+            array(components, bins),
+        ],
         "time_pass",
-        [WHOLE] * 7,
+        [WHOLE] * 6,
         5,
         [
             pltpu.VMEM((tri * trials, components), f32),
-            pltpu.VMEM((components, components), f32),
             pltpu.SemaphoreType.DMA((3,)),
         ],
         [in_hbm] * 3 + [WHOLE],
-    )(ours, theirs, inverse_two, gram_neuron, flipped, held(spikes), held(new))
+    )(ours, theirs, inverse_two, flipped, held(spikes), held(new))
     pieces = lax.all_to_all(time_part.reshape(neu * tri, components // (neu * tri), bins), both, 0, 0)
-    (inverse_three,) = call(third_system, [square], "third_system", [WHOLE], 4, work)(system_three)
+    (inverse_three,) = call(third_system, [square], "third_system", [WHOLE] * 2, 4, work)(gram_neuron, trial_table)
     piece = jnp.sum(pieces, axis=0, keepdims=True)
     mttkrp_time = lax.all_to_all(jnp.broadcast_to(piece, pieces.shape), both, 0, 0).reshape(components, bins)
     time_new, weights = call(time_solve, [array(bins, components), array(1, components)], "time_solve", [WHOLE] * 2)(

time: 125 us -> 124 us (level)
  no operation moved by 1% of the time
where the time goes in v4:
time: 124 us
  blocking collectives  81.1 us (65%)
  Pallas kernels  22.9 us (18%)
  starting transfers between devices  11.3 us (9%)
  waiting for transfers between devices  7.01 us (6%)
    all_to_all x1, blocking collectives, body(): parts = lax.all_to_all(part, 'tri', 0, 0)  21.9 us
    all_to_all x1, blocking collectives, body(): gathered = lax.all_to_all(trial_part, both, 0, 0, axis_index_groups=groups)  17.8 us
    all_to_all x1, blocking collectives, body(): raw = lax.all_to_all(copies, 'tri', 0, 0).reshape(rows, components)  15.5 us
    all_to_all x1, blocking collectives, body(): lax.all_to_all(time_part.reshape(neu * tri, components // (neu * tri), bi...  13 us
    all_to_all x1, blocking collectives, body(): grams = lax.all_to_all(packed, 'neu', 0, 0, axis_index_groups=groups)  12.9 us
    pallas_call x1, Pallas kernels, body(): call(neuron_pass, [pltpu.VMEM(spike_counts.shape, bf16), pltpu.VMEM((tria...  7.35 us
    all_to_all x1, waiting for transfers between devices, body(): lax.all_to_all(jnp.broadcast_to(piece, pieces.shape), both, 0, 0)  6.11 us
    all_to_all x1, starting transfers between devices, body(): lax.all_to_all(jnp.broadcast_to(piece, pieces.shape), both, 0, 0)  4.26 us
  transfers between devices with their start and end apart: 3, of which 2 were waited for; matrix products, arithmetic and copies ran while one was open for 0% of the time, Pallas kernels for 5%

profile of v4, /device:TPU:1, one launch (start us, length us, event | category | flops | bytes accessed | tf_op | source)
XLA Modules:
  0.0 124.1 jit_solution(13074663342556356648)
XLA Ops:
  0.6 0.0 copy-start
  0.6 7.3 %neuron_pass.1 = (bf16[16,2048,256]{2,1,0:T(8,128)(2,1)S(1)}, f32[16,2048,128]{2,1,0:T(8,128)S(1)}, f32[8,272,128]{2,1,0:T(8,128)S(1)}) custom-call(bf16[16,2048,256]{2,1,0:T(8,128)(2,1)} %spikes_hbm.1, bf16[256,128]{1,0:T(8,128)(2,1)} %time_ref.1, bf16[16,128]{1,0:T(8,128)(2,1)} %trial_hbm.1), custom_call_target="tpu_custom_call" | custom-call | tf_op jit(solution)/shard_map/neuron_pass/pallas_call | solution.py:308
  8.0 21.9 %all_to_all.30.parts_ref = f32[8,272,128]{2,1,0:T(8,128)S(1)} all-to-all(f32[8,272,128]{2,1,0:T(8,128)S(1)} %get-tuple-element.20), channel_id=1, replica_groups=mesh['neu'=16,'tri'=8] {'tri'}, dimensions={0} | all-to-all | bytes 2228224 | tf_op jit(solution)/shard_map/all_to_all | solution.py:324
  29.9 0.0 copy-done
  29.9 3.1 %neuron_solve.1 = (f32[8,256,128]{2,1,0:T(8,128)S(1)}, f32[128,128]{1,0:T(8,128)S(1)}) custom-call(f32[8,272,128]{2,1,0:T(8,128)S(1)} %all_to_all.30.parts_ref, bf16[256,128]{1,0:T(8,128)(2,1)S(1)} %copy-done, f32[16,2048,128]{2,1,0:T(8,128)S(1)} %get-tuple-element.21.held_ref.refs_2_, ...), custom_call_target="tpu_custom_call" | custom-call | tf_op jit(solution)/shard_map/neuron_solve/pallas_call | solution.py:325
  33.0 15.5 %all_to_all.31 = f32[8,256,128]{2,1,0:T(8,128)S(1)} all-to-all(f32[8,256,128]{2,1,0:T(8,128)S(1)} %get-tuple-element.23), channel_id=1, replica_groups=mesh['neu'=16,'tri'=8] {'tri'}, dimensions={0} | all-to-all | bytes 2097152 | tf_op jit(solution)/shard_map/all_to_all | solution.py:333
  48.5 0.5 neuron_gram.1.ours_ref
  49.0 3.8 %collective-permute-start = (f32[128,128]{1,0:T(8,128)S(1)}, f32[128,128]{1,0:T(8,128)S(1)}, u32[]{:S(2)}, u32[]{:S(2)}) collective-permute-start(f32[128,128]{1,0:T(8,128)S(1)} %neuron_gram.1.ours_ref), channel_id=1, source_target_pairs={{0,8},{8,0},{16,24},{24,16},{32,40},{40,32},{48,56},{56,48},{64,72... | collective-permute-start | bytes 196616 | tf_op jit(solution)/shard_map/ppermute | solution.py:337
  52.8 0.9 collective-permute-done.theirs_ref
  53.7 12.9 %all_to_all.32.refs_0_ = f32[8,24,128]{2,1,0:T(8,128)S(1)} all-to-all(f32[8,24,128]{2,1,0:T(8,128)S(1)} %pack_gram.1), channel_id=1, replica_groups={{0,16,32,48,64,80,96,112},{8,24,40,56,72,88,104,120},{1,17,33,49,65,81,..., dimensions={0} | all-to-all | bytes 196608 | tf_op jit(solution)/shard_map/all_to_all | solution.py:339
  66.6 1.6 %trial_pass.1 = (f32[2048,128]{1,0:T(8,128)S(1)}, f32[128,2048]{1,0:T(8,128)S(1)}, f32[64,24,128]{2,1,0:T(8,128)S(1)}) custom-call(f32[8,24,128]{2,1,0:T(8,128)S(1)} %all_to_all.32.refs_0_, f32[2048,128]{1,0:T(8,128)S(1)} %bitcast.7, f32[16,2048,128]{2,1,0:T(8,128)S(1)} %get-tuple-element.21.held_ref.refs_2_, ...), custom_call_target="tpu_custom_call" | custom-call | tf_op jit(solution)/shard_map/trial_pass/pallas_call | solution.py:340
  68.2 17.8 %all_to_all.33.gathered_ref.refs_1_ = f32[64,24,128]{2,1,0:T(8,128)S(1)} all-to-all(f32[64,24,128]{2,1,0:T(8,128)S(1)} %get-tuple-element.24), channel_id=1, replica_groups={{0,1,2,3,4,5,6,7,16,17,18,19,20,21,22,23,32,33,34,35,36,37,38,39,48,49,..., dimensions={0} | all-to-all | bytes 1572864 | tf_op jit(solution)/shard_map/all_to_all | solution.py:353
  86.1 3.2 %collective-permute-start.1 = (f32[128,128]{1,0:T(8,128)S(1)}, f32[128,128]{1,0:T(8,128)S(1)}, u32[]{:S(2)}, u32[]{:S(2)}) collective-permute-start(f32[128,128]{1,0:T(8,128)S(1)} %trial_sum.1.ours_ref), channel_id=1, source_target_pairs={{0,8},{8,0},{16,24},{24,16},{32,40},{40,32},{48,56},{56,48},{64,72... | collective-permute-start | bytes 196616 | tf_op jit(solution)/shard_map/ppermute | solution.py:355
  89.3 2.5 %second_system.1 = (f32[128,128]{1,0:T(8,128)S(1)}, f32[128,128]{1,0:T(8,128)S(1)}) custom-call(f32[128,128]{1,0:T(8,128)S(1)} %get-tuple-element.25.refs_0_, f32[64,24,128]{2,1,0:T(8,128)S(1)} %all_to_all.33.gathered_ref.refs_1_, bf16[16,2048,256]{2,1,0:T(8,128)(2,1)S(1)} %get-tuple-element.22.kept_ref.refs_3_.refs_2_.spikes_ref), custom_call_target="tpu_custom_call" | custom-call | tf_op jit(solution)/shard_map/second_system/pallas_call | solution.py:356
  91.8 0.0 collective-permute-done.1.theirs_ref
  91.8 2.8 %time_pass.1 = (f32[2048,128]{1,0:T(8,128)}, f32[16,128]{1,0:T(8,128)}, f32[128,128]{1,0:T(8,128)S(1)}, f32[128,256]{1,0:T(8,128)S(1)}) custom-call(f32[128,128]{1,0:T(8,128)S(1)} %trial_sum.1.ours_ref, f32[128,128]{1,0:T(8,128)S(1)} %collective-permute-done.1.theirs_ref, f32[128,128]{1,0:T(8,128)S(1)} %get-tuple-element.26.inverse_ref, ...), custom_call_target="tpu_custom_call" | custom-call | tf_op jit(solution)/shard_map/time_pass/pallas_call | solution.py:359
  94.6 0.1 copy.7
  94.8 13.0 %all_to_all.34 = f32[128,1,256]{2,1,0:T(1,128)S(1)} all-to-all(f32[128,1,256]{2,1,0:T(1,128)S(1)} %copy.7), channel_id=1, replica_groups=mesh['neu'=16,'tri'=8] {'neu','tri'}, dimensions={0} | all-to-all | bytes 262144 | tf_op jit(solution)/shard_map/all_to_all | solution.py:376
  107.8 0.2 reduce_sum.9
  108.0 0.7 broadcast_in_dim.2
  108.7 4.3 %all-to-all-start.5 = ((f32[128,1,256]{2,1,0:T(1,128)}), f32[128,1,256]{2,1,0:T(1,128)S(1)}, u32[]{:S(2)}, u32[]{:S(2)}) async-start(f32[128,1,256]{2,1,0:T(1,128)} %broadcast_in_dim.2), calls=%async_computation.5 | async-start | bytes 262144 | tf_op jit(solution)/shard_map/all_to_all | solution.py:379
  113.0 4.0 %third_system.1.inverse_ref = f32[128,128]{1,0:T(8,128)S(1)} custom-call(f32[128,128]{1,0:T(8,128)S(1)} %get-tuple-element.32.gram_neuron_ref, f32[128,128]{1,0:T(8,128)S(1)} %get-tuple-element.33.table_ref), custom_call_target="tpu_custom_call" | custom-call | tf_op jit(solution)/shard_map/third_system/pallas_call | solution.py:377
  116.9 6.1 %all-to-all-done.5 = f32[128,1,256]{2,1,0:T(1,128)S(1)} async-done(((f32[128,1,256]{2,1,0:T(1,128)}), f32[128,1,256]{2,1,0:T(1,128)S(1)}, u32[]{:S(2)}, u32[]{:S(2)}) %all-to-all-start.5) | async-done | bytes 131104 | tf_op jit(solution)/shard_map/all_to_all | solution.py:379
  123.1 1.0 time_solve.1
  (3 shorter events, 0.1 us)
Async XLA Ops:
  0.6 29.2 %copy-start = (bf16[256,128]{1,0:T(8,128)(2,1)S(1)}, bf16[256,128]{1,0:T(8,128)(2,1)}, u32[]{:S(2)}) copy-start(bf16[256,128]{1,0:T(8,128)(2,1)} %time_ref.1) | copy-start | bytes 196612
  49.0 4.7 %collective-permute-start = (f32[128,128]{1,0:T(8,128)S(1)}, f32[128,128]{1,0:T(8,128)S(1)}, u32[]{:S(2)}, u32[]{:S(2)}) collective-permute-start(f32[128,128]{1,0:T(8,128)S(1)} %neuron_gram.1.ours_ref), channel_id=1, source_target_pairs={{0,8},{8,0},{16,24},{24,16},{32,40},{40,32},{48,56},{56,48},{64,72... | collective-permute-start | bytes 196616 | tf_op jit(solution)/shard_map/ppermute | solution.py:337
  86.1 5.7 %collective-permute-start.1 = (f32[128,128]{1,0:T(8,128)S(1)}, f32[128,128]{1,0:T(8,128)S(1)}, u32[]{:S(2)}, u32[]{:S(2)}) collective-permute-start(f32[128,128]{1,0:T(8,128)S(1)} %trial_sum.1.ours_ref), channel_id=1, source_target_pairs={{0,8},{8,0},{16,24},{24,16},{32,40},{40,32},{48,56},{56,48},{64,72... | collective-permute-start | bytes 196616 | tf_op jit(solution)/shard_map/ppermute | solution.py:355
  108.7 14.3 %all-to-all-start.5 = ((f32[128,1,256]{2,1,0:T(1,128)}), f32[128,1,256]{2,1,0:T(1,128)S(1)}, u32[]{:S(2)}, u32[]{:S(2)}) async-start(f32[128,1,256]{2,1,0:T(1,128)} %broadcast_in_dim.2), calls=%async_computation.5 | async-start | bytes 262144 | tf_op jit(solution)/shard_map/all_to_all | solution.py:379

commit v5 on v4

--- a/solution.py
+++ b/solution.py
@@ -147,8 +147,8 @@
 
 
 def neuron_solve(parts_ref, time_ref, held_ref, kept_ref, copies_ref, gram_time_ref, trial_ref, *work):
-    blocks, rows, _ = copies_ref.shape
-    extended = parts_ref.shape[1]
+    blocks, extended, _ = parts_ref.shape
+    rows = copies_ref.shape[1]
     trials = extended - rows
     total = parts_ref[0, 0:rows, :]
     for b in range(1, blocks):
@@ -160,7 +160,7 @@
     gram_trial = lax.dot_general(trial_ref[...], trial_ref[...], across, preferred_element_type=f32)
     gram_time_ref[...] = gram_time
     raw = dot(total, inverse(gram_time * gram_trial, *work))
-    for b in range(blocks):
+    for b in range(copies_ref.shape[0]):
         copies_ref[b] = raw
 
 
@@ -188,24 +188,29 @@
     )
 
 
-def trial_pass(count, grams_ref, raw_ref, projected_ref, kept_ref, new_ref, flipped_ref, part_ref, half_ref):
+def trial_pass(count, grams_ref, ours_ref, theirs_ref, projected_ref, kept_ref, new_ref, flipped_ref, part_ref, half_ref):
     trials, rows, components = projected_ref.shape
-    tri = lax.axis_size("tri")
+    ring = lax.axis_size("tri") // 2
     gram = jnp.sum(grams_ref[...], axis=0)
-    lines = components // grams_ref.shape[0]
+    lines = grams_ref.shape[1] - PAD
     scale = jnp.sqrt(gram[lines : lines + 1, :] / count + 1e-06)
-    share = lines // tri
-    first = lax.axis_index("tri") * share
+    share = lines // ring
+    here = lax.axis_index("tri")
+    first = lax.rem(here, ring) * share
     place = lax.broadcasted_iota(jnp.int32, (lines, components), 0)
     spot = lax.broadcasted_iota(jnp.int32, (PAD, components), 0)
     sent = jnp.zeros((PAD, components), f32)
     for i in range(share):
         line = jnp.sum(jnp.where(place == first + i, gram[0:lines, :], 0.0), axis=0, keepdims=True)
         sent = jnp.where(spot == i, line, sent)
-    new = raw_ref[...] * (1.0 / scale)
-    new_ref[...] = new
-    flipped_ref[...] = new.T
-    half_ref[...] = new.astype(bf16).astype(f32)
+    ratio = 1.0 / scale
+    for side, raw_ref in enumerate((ours_ref, theirs_ref)):
+        count_rows = raw_ref.shape[0]
+        span = pl.ds(pl.multiple_of(lax.rem(here // ring + side, 2) * count_rows, count_rows), count_rows)
+        new = raw_ref[...] * ratio
+        new_ref[span, :] = new
+        flipped_ref[:, span] = new.T
+        half_ref[span, :] = new.astype(bf16).astype(f32)
     block = 64
 
     def step(b, totals):
@@ -299,6 +304,7 @@
     block = rows // tri
     half = neu // 2
     both = ("neu", "tri")
+    ring = tri // 2
     swap = [(i, i ^ 1) for i in range(neu)]
     in_hbm = pl.BlockSpec(memory_space=pltpu.HBM)
 
@@ -324,19 +330,23 @@
     parts = lax.all_to_all(part, "tri", 0, 0)
     copies, gram_time = call(
         neuron_solve,
-        [array(tri, block, components), square],
+        [array(ring, block, components), square],
         "neuron_solve",
         [WHOLE] * 4,
         5,
         [pltpu.VMEM((tri * trials, components), bf16)] + work,
     )(parts, time_factor, held(projected), held(spikes))
-    raw = lax.all_to_all(copies, "tri", 0, 0).reshape(rows, components)
-    (gram_part,) = call(neuron_gram, [square], "neuron_gram", [WHOLE] * 3)(raw, held(projected), held(spikes))
+    rings = [list(range(x * ring, (x + 1) * ring)) for x in range(2)]
+    near = lax.all_to_all(copies, "tri", 0, 0, axis_index_groups=rings).reshape(rows // 2, components)
+    far = lax.ppermute(near, "tri", [(t, (t + ring) % tri) for t in range(tri)])
+    (gram_part,) = call(neuron_gram, [square], "neuron_gram", [WHOLE] * 3)(near, held(projected), held(spikes))
     (packed,) = call(
-        pack_gram, [array(half, components // half + PAD, components)], "pack_gram", [WHOLE] * 2
+        pack_gram, [array(neu, components // neu + PAD, components)], "pack_gram", [WHOLE] * 2
     )(gram_part, lax.ppermute(gram_part, "neu", swap))
-    groups = [list(range(c, neu, 2)) for c in range(2)]
-    grams = lax.all_to_all(packed, "neu", 0, 0, axis_index_groups=groups)
+    groups = [
+        [n * tri + x * ring + z for n in range(c, neu, 2) for x in range(2)] for c in range(2) for z in range(ring)
+    ]
+    grams = lax.all_to_all(packed, both, 0, 0, axis_index_groups=groups)
     new, flipped, trial_part = call(
         lambda *refs: trial_pass(neu * rows, *refs),
         [
@@ -345,10 +355,10 @@
             array(half * tri, trials + PAD, components),
         ],
         "trial_pass",
-        [WHOLE] * 4,
+        [WHOLE] * 5,
         5,
         [pltpu.VMEM((rows, components), f32)],
-    )(grams, raw, held(projected), held(spikes))
+    )(grams, near, far, held(projected), held(spikes))
     groups = [[n * tri + t for n in range(c, neu, 2) for t in range(tri)] for c in range(2)]
     gathered = lax.all_to_all(trial_part, both, 0, 0, axis_index_groups=groups)
     (ours,) = call(trial_sum, [array(tri * trials, components)], "trial_sum", [WHOLE] * 2)(gathered, held(spikes))

time: 124 us -> 120 us (0.968)
  blocking collectives: 81.1 us -> 75.9 us
    all_to_all x2, blocking collectives: 28.4 us -> 22.4 us  [the longest x1 13.1 us: body(): grams = lax.all_to_all(packed, both, 0, 0, axis_index_groups=groups)]
  transfers between devices with their start and end apart: 3 -> 4, of which waited for: 2 -> 2; matrix products, arithmetic and copies ran while one was open for 0% -> 0% of each run, Pallas kernels for 5% -> 6%
where the time goes in v5:
time: 120 us
  blocking collectives  75.9 us (63%)
  Pallas kernels  23.6 us (20%)
  starting transfers between devices  11.7 us (10%)
  waiting for transfers between devices  6.63 us (6%)
    all_to_all x1, blocking collectives, body(): parts = lax.all_to_all(part, 'tri', 0, 0)  21.9 us
    all_to_all x1, blocking collectives, body(): gathered = lax.all_to_all(trial_part, both, 0, 0, axis_index_groups=groups)  18.5 us
    all_to_all x1, blocking collectives, body(): grams = lax.all_to_all(packed, both, 0, 0, axis_index_groups=groups)  13.1 us
    all_to_all x1, blocking collectives, body(): lax.all_to_all(time_part.reshape(neu * tri, components // (neu * tri), bi...  13 us
    all_to_all x1, blocking collectives, body(): lax.all_to_all(copies, 'tri', 0, 0, axis_index_groups=rings)  9.36 us
    pallas_call x1, Pallas kernels, body(): call(neuron_pass, [pltpu.VMEM(spike_counts.shape, bf16), pltpu.VMEM((tria...  7.35 us
    all_to_all x1, waiting for transfers between devices, body(): lax.all_to_all(jnp.broadcast_to(piece, pieces.shape), both, 0, 0)  5.72 us
    pallas_call x1, Pallas kernels, body(): call(third_system, [square], 'third_system', [WHOLE] * 2, 4, work)  4.35 us
  transfers between devices with their start and end apart: 4, of which 2 were waited for; matrix products, arithmetic and copies ran while one was open for 0% of the time, Pallas kernels for 6%

profile of v5, /device:TPU:1, one launch (start us, length us, event | category | flops | bytes accessed | tf_op | source)
XLA Modules:
  0.0 119.6 jit_solution(17525030904632127681)
XLA Ops:
  0.6 0.0 copy-start
  0.6 7.3 %neuron_pass.1 = (bf16[16,2048,256]{2,1,0:T(8,128)(2,1)S(1)}, f32[16,2048,128]{2,1,0:T(8,128)S(1)}, f32[8,272,128]{2,1,0:T(8,128)S(1)}) custom-call(bf16[16,2048,256]{2,1,0:T(8,128)(2,1)} %spikes_hbm.1, bf16[256,128]{1,0:T(8,128)(2,1)} %time_ref.1, bf16[16,128]{1,0:T(8,128)(2,1)} %trial_hbm.1), custom_call_target="tpu_custom_call" | custom-call | tf_op jit(solution)/shard_map/neuron_pass/pallas_call | solution.py:314
  8.0 21.9 %all_to_all.30.parts_ref = f32[8,272,128]{2,1,0:T(8,128)S(1)} all-to-all(f32[8,272,128]{2,1,0:T(8,128)S(1)} %get-tuple-element.20), channel_id=1, replica_groups=mesh['neu'=16,'tri'=8] {'tri'}, dimensions={0} | all-to-all | bytes 2228224 | tf_op jit(solution)/shard_map/all_to_all | solution.py:330
  29.9 0.0 copy-done
  29.9 3.1 %neuron_solve.1 = (f32[4,256,128]{2,1,0:T(8,128)S(1)}, f32[128,128]{1,0:T(8,128)S(1)}) custom-call(f32[8,272,128]{2,1,0:T(8,128)S(1)} %all_to_all.30.parts_ref, bf16[256,128]{1,0:T(8,128)(2,1)S(1)} %copy-done, f32[16,2048,128]{2,1,0:T(8,128)S(1)} %get-tuple-element.21.held_ref.refs_3_, ...), custom_call_target="tpu_custom_call" | custom-call | tf_op jit(solution)/shard_map/neuron_solve/pallas_call | solution.py:331
  32.9 9.4 %all_to_all.31 = f32[4,256,128]{2,1,0:T(8,128)S(1)} all-to-all(f32[4,256,128]{2,1,0:T(8,128)S(1)} %get-tuple-element.23), channel_id=1, replica_groups={{0,1,2,3},{4,5,6,7},{8,9,10,11},{12,13,14,15},{16,17,18,19},{20,21,22,2..., dimensions={0} | all-to-all | bytes 1048576 | tf_op jit(solution)/shard_map/all_to_all | solution.py:340
  42.3 0.6 collective-permute-start.1
  42.9 0.3 neuron_gram.1.ours_ref
  43.2 3.7 %collective-permute-start = (f32[128,128]{1,0:T(8,128)S(1)}, f32[128,128]{1,0:T(8,128)S(1)}, u32[]{:S(2)}, u32[]{:S(2)}) collective-permute-start(f32[128,128]{1,0:T(8,128)S(1)} %neuron_gram.1.ours_ref), channel_id=1, source_target_pairs={{0,8},{8,0},{16,24},{24,16},{32,40},{40,32},{48,56},{56,48},{64,72... | collective-permute-start | bytes 196616 | tf_op jit(solution)/shard_map/ppermute | solution.py:345
  46.9 0.9 collective-permute-done.theirs_ref
  47.9 13.1 %all_to_all.32.refs_0_ = f32[16,16,128]{2,1,0:T(8,128)S(1)} all-to-all(f32[16,16,128]{2,1,0:T(8,128)S(1)} %pack_gram.1), channel_id=1, replica_groups={{0,4,16,20,32,36,48,52,64,68,80,84,96,100,112,116},{1,5,17,21,33,37,49,..., dimensions={0} | all-to-all | bytes 262144 | tf_op jit(solution)/shard_map/all_to_all | solution.py:349
  61.0 0.0 collective-permute-done.1.refs_2_
  61.0 1.7 %trial_pass.1 = (f32[2048,128]{1,0:T(8,128)S(1)}, f32[128,2048]{1,0:T(8,128)S(1)}, f32[64,24,128]{2,1,0:T(8,128)S(1)}) custom-call(f32[16,16,128]{2,1,0:T(8,128)S(1)} %all_to_all.32.refs_0_, f32[1024,128]{1,0:T(8,128)S(1)} %bitcast.8, f32[1024,128]{1,0:T(8,128)S(1)} %collective-permute-done.1.refs_2_, ...), custom_call_target="tpu_custom_call" | custom-call | tf_op jit(solution)/shard_map/trial_pass/pallas_call | solution.py:350
  62.6 18.5 %all_to_all.33.gathered_ref.refs_1_ = f32[64,24,128]{2,1,0:T(8,128)S(1)} all-to-all(f32[64,24,128]{2,1,0:T(8,128)S(1)} %get-tuple-element.24), channel_id=1, replica_groups={{0,1,2,3,4,5,6,7,16,17,18,19,20,21,22,23,32,33,34,35,36,37,38,39,48,49,..., dimensions={0} | all-to-all | bytes 1572864 | tf_op jit(solution)/shard_map/all_to_all | solution.py:363
  81.2 3.2 %collective-permute-start.2 = (f32[128,128]{1,0:T(8,128)S(1)}, f32[128,128]{1,0:T(8,128)S(1)}, u32[]{:S(2)}, u32[]{:S(2)}) collective-permute-start(f32[128,128]{1,0:T(8,128)S(1)} %trial_sum.1.ours_ref), channel_id=1, source_target_pairs={{0,8},{8,0},{16,24},{24,16},{32,40},{40,32},{48,56},{56,48},{64,72... | collective-permute-start | bytes 196616 | tf_op jit(solution)/shard_map/ppermute | solution.py:365
  84.4 2.9 %second_system.1 = (f32[128,128]{1,0:T(8,128)S(1)}, f32[128,128]{1,0:T(8,128)S(1)}) custom-call(f32[128,128]{1,0:T(8,128)S(1)} %get-tuple-element.25.refs_0_, f32[64,24,128]{2,1,0:T(8,128)S(1)} %all_to_all.33.gathered_ref.refs_1_, bf16[16,2048,256]{2,1,0:T(8,128)(2,1)S(1)} %get-tuple-element.22.kept_ref.refs_4_.refs_2_.spikes_ref), custom_call_target="tpu_custom_call" | custom-call | tf_op jit(solution)/shard_map/second_system/pallas_call | solution.py:366
  87.3 0.0 collective-permute-done.2.theirs_ref
  87.3 2.8 %time_pass.1 = (f32[2048,128]{1,0:T(8,128)}, f32[16,128]{1,0:T(8,128)}, f32[128,128]{1,0:T(8,128)S(1)}, f32[128,256]{1,0:T(8,128)S(1)}) custom-call(f32[128,128]{1,0:T(8,128)S(1)} %trial_sum.1.ours_ref, f32[128,128]{1,0:T(8,128)S(1)} %collective-permute-done.2.theirs_ref, f32[128,128]{1,0:T(8,128)S(1)} %get-tuple-element.26.inverse_ref, ...), custom_call_target="tpu_custom_call" | custom-call | tf_op jit(solution)/shard_map/time_pass/pallas_call | solution.py:369
  90.1 0.1 copy.7
  90.3 13.0 %all_to_all.34 = f32[128,1,256]{2,1,0:T(1,128)S(1)} all-to-all(f32[128,1,256]{2,1,0:T(1,128)S(1)} %copy.7), channel_id=1, replica_groups=mesh['neu'=16,'tri'=8] {'neu','tri'}, dimensions={0} | all-to-all | bytes 262144 | tf_op jit(solution)/shard_map/all_to_all | solution.py:386
  103.3 0.2 reduce_sum.9
  103.5 0.7 broadcast_in_dim.2
  104.2 4.3 %all-to-all-start.5 = ((f32[128,1,256]{2,1,0:T(1,128)}), f32[128,1,256]{2,1,0:T(1,128)S(1)}, u32[]{:S(2)}, u32[]{:S(2)}) async-start(f32[128,1,256]{2,1,0:T(1,128)} %broadcast_in_dim.2), calls=%async_computation.5 | async-start | bytes 262144 | tf_op jit(solution)/shard_map/all_to_all | solution.py:389
  108.5 4.4 %third_system.1.inverse_ref = f32[128,128]{1,0:T(8,128)S(1)} custom-call(f32[128,128]{1,0:T(8,128)S(1)} %get-tuple-element.32.gram_neuron_ref, f32[128,128]{1,0:T(8,128)S(1)} %get-tuple-element.33.table_ref), custom_call_target="tpu_custom_call" | custom-call | tf_op jit(solution)/shard_map/third_system/pallas_call | solution.py:387
  112.8 5.7 %all-to-all-done.5 = f32[128,1,256]{2,1,0:T(1,128)S(1)} async-done(((f32[128,1,256]{2,1,0:T(1,128)}), f32[128,1,256]{2,1,0:T(1,128)S(1)}, u32[]{:S(2)}, u32[]{:S(2)}) %all-to-all-start.5) | async-done | bytes 131104 | tf_op jit(solution)/shard_map/all_to_all | solution.py:389
  118.6 1.0 time_solve.1
  (3 shorter events, 0.1 us)
Async XLA Ops:
  0.6 29.2 %copy-start = (bf16[256,128]{1,0:T(8,128)(2,1)S(1)}, bf16[256,128]{1,0:T(8,128)(2,1)}, u32[]{:S(2)}) copy-start(bf16[256,128]{1,0:T(8,128)(2,1)} %time_ref.1) | copy-start | bytes 196612
  42.3 18.7 %collective-permute-start.1 = (f32[1024,128]{1,0:T(8,128)S(1)}, f32[1024,128]{1,0:T(8,128)S(1)}, u32[]{:S(2)}, u32[]{:S(2)}) collective-permute-start(f32[1024,128]{1,0:T(8,128)S(1)} %bitcast.6), channel_id=1, source_target_pairs={{0,4},{1,5},{2,6},{3,7},{4,0},{5,1},{6,2},{7,3},{8,12},{9,13},{10,... | collective-permute-start | bytes 1572872 | tf_op jit(solution)/shard_map/ppermute | solution.py:341
  43.2 4.6 %collective-permute-start = (f32[128,128]{1,0:T(8,128)S(1)}, f32[128,128]{1,0:T(8,128)S(1)}, u32[]{:S(2)}, u32[]{:S(2)}) collective-permute-start(f32[128,128]{1,0:T(8,128)S(1)} %neuron_gram.1.ours_ref), channel_id=1, source_target_pairs={{0,8},{8,0},{16,24},{24,16},{32,40},{40,32},{48,56},{56,48},{64,72... | collective-permute-start | bytes 196616 | tf_op jit(solution)/shard_map/ppermute | solution.py:345
  81.2 6.1 %collective-permute-start.2 = (f32[128,128]{1,0:T(8,128)S(1)}, f32[128,128]{1,0:T(8,128)S(1)}, u32[]{:S(2)}, u32[]{:S(2)}) collective-permute-start(f32[128,128]{1,0:T(8,128)S(1)} %trial_sum.1.ours_ref), channel_id=1, source_target_pairs={{0,8},{8,0},{16,24},{24,16},{32,40},{40,32},{48,56},{56,48},{64,72... | collective-permute-start | bytes 196616 | tf_op jit(solution)/shard_map/ppermute | solution.py:365
  104.2 14.3 %all-to-all-start.5 = ((f32[128,1,256]{2,1,0:T(1,128)}), f32[128,1,256]{2,1,0:T(1,128)S(1)}, u32[]{:S(2)}, u32[]{:S(2)}) async-start(f32[128,1,256]{2,1,0:T(1,128)} %broadcast_in_dim.2), calls=%async_computation.5 | async-start | bytes 262144 | tf_op jit(solution)/shard_map/all_to_all | solution.py:389

commit v6 on v5

--- a/solution.py
+++ b/solution.py
@@ -110,51 +110,64 @@
     return approx * left * right
 
 
-def neuron_pass(spikes_hbm, time_hbm, trial_hbm, spikes_ref, projected_ref, part_ref, time_ref, trial_ref, sems):
-    trials = projected_ref.shape[0]
-    blocks, extended, _ = part_ref.shape
-    rows = extended - trials
+def neuron_pass(
+    far, spikes_hbm, time_hbm, trial_hbm, *refs
+):
+    if not far:
+        refs = refs[2:]
+    spikes_ref, projected_ref, *part_refs, time_ref, trial_ref, sems = refs
+    trials, total_rows, _ = projected_ref.shape
+    ring = lax.axis_size("tri") // 2
+    rows = total_rows // ring
+    half, here = lax.axis_index("tri") // ring, lax.rem(lax.axis_index("tri"), ring)
+    first = (lax.rem(half + 1, 2) if far else half) * total_rows
     small = [
-        pltpu.make_async_copy(time_hbm, time_ref, sems.at[blocks]),
-        pltpu.make_async_copy(trial_hbm, trial_ref, sems.at[blocks + 1]),
+        pltpu.make_async_copy(time_hbm, time_ref, sems.at[ring]),
+        pltpu.make_async_copy(trial_hbm, trial_ref, sems.at[ring + 1]),
     ]
     for copy in small:
         copy.start()
-    copies = []
-    for b in range(blocks):
-        span = pl.ds(b * rows, rows)
+    spans, copies = [], []
+    for b in range(ring):
+        place = lax.rem(here + b, ring) * rows
+        span = pl.ds(pl.multiple_of(place, rows), rows)
+        source = pl.ds(pl.multiple_of(first + place, rows), rows)
+        spans.append(span)
         copies.append(
-            pltpu.make_async_copy(spikes_hbm.at[:, span, :], spikes_ref.at[:, span, :], sems.at[b])
+            pltpu.make_async_copy(spikes_hbm.at[:, source, :], spikes_ref.at[:, span, :], sems.at[b])
         )
-    for b in range(min(AHEAD, blocks)):
-        copies[b].start()
+    for copy in copies[:AHEAD]:
+        copy.start()
     for copy in small:
         copy.wait()
     trial = trial_ref[...].astype(f32)
-    for b in range(blocks):
+    for b in range(ring):
         copies[b].wait()
-        if b + AHEAD < blocks:
+        if b + AHEAD < ring:
             copies[b + AHEAD].start()
-        span = pl.ds(b * rows, rows)
         total = None
         for k in range(trials):
-            projected = jnp.dot(spikes_ref[k, span, :], time_ref[...], preferred_element_type=f32)
-            projected_ref[k, span, :] = projected
+            projected = jnp.dot(spikes_ref[k, spans[b], :], time_ref[...], preferred_element_type=f32)
+            projected_ref[k, spans[b], :] = projected
             term = projected * trial[k : k + 1, :]
             total = term if total is None else total + term
-        part_ref[b, 0:rows, :] = total
-        part_ref[b, rows:extended, :] = trial
-
-
-def neuron_solve(parts_ref, time_ref, held_ref, kept_ref, copies_ref, gram_time_ref, trial_ref, *work):
-    blocks, extended, _ = parts_ref.shape
-    rows = copies_ref.shape[1]
+        part_ref = part_refs[b]
+        part_ref[0:rows, :] = total
+        part_ref[rows : rows + trials, :] = trial
+
+
+def neuron_solve(*refs):
+    blocks = lax.axis_size("tri")
+    parts, refs = refs[:blocks], refs[blocks:]
+    time_ref, *_, copies_ref, gram_time_ref, trial_ref, scaled_ref, approx_ref, error_ref = refs
+    work = scaled_ref, approx_ref, error_ref
+    extended, rows = parts[0].shape[0], copies_ref.shape[1]
     trials = extended - rows
-    total = parts_ref[0, 0:rows, :]
-    for b in range(1, blocks):
-        total = total + parts_ref[b, 0:rows, :]
-    for b in range(blocks):
-        trial_ref[b * trials : (b + 1) * trials, :] = parts_ref[b, rows:extended, :].astype(bf16)
+    total = parts[0][0:rows, :]
+    for part in parts[1:]:
+        total = total + part[0:rows, :]
+    for b, part in enumerate(parts):
+        trial_ref[b * trials : (b + 1) * trials, :] = part[rows:extended, :].astype(bf16)
     across = (((0,), (0,)), ((), ()))
     gram_time = lax.dot_general(time_ref[...], time_ref[...], across, preferred_element_type=f32)
     gram_trial = lax.dot_general(trial_ref[...], trial_ref[...], across, preferred_element_type=f32)
@@ -174,7 +187,8 @@
         packed_ref[d, rows:extended, :] = jnp.broadcast_to(diagonal, (extended - rows, components))
 
 
-def neuron_gram(raw_ref, held_ref, kept_ref, gram_ref):
+def neuron_gram(raw_ref, *refs):
+    gram_ref = refs[-1]
     components = raw_ref.shape[1]
     raw = raw_ref[...]
     upper = raw.astype(bf16)
@@ -188,8 +202,9 @@
     )
 
 
-def trial_pass(count, grams_ref, ours_ref, theirs_ref, projected_ref, kept_ref, new_ref, flipped_ref, part_ref, half_ref):
-    trials, rows, components = projected_ref.shape
+def trial_pass(count, grams_ref, ours_ref, theirs_ref, near_ref, far_ref, *refs):
+    *_, new_ref, flipped_ref, part_ref, half_ref = refs
+    trials, rows, components = near_ref.shape
     ring = lax.axis_size("tri") // 2
     gram = jnp.sum(grams_ref[...], axis=0)
     lines = grams_ref.shape[1] - PAD
@@ -205,31 +220,33 @@
         sent = jnp.where(spot == i, line, sent)
     ratio = 1.0 / scale
     for side, raw_ref in enumerate((ours_ref, theirs_ref)):
-        count_rows = raw_ref.shape[0]
-        span = pl.ds(pl.multiple_of(lax.rem(here // ring + side, 2) * count_rows, count_rows), count_rows)
+        span = slice(side * rows, (side + 1) * rows)
         new = raw_ref[...] * ratio
         new_ref[span, :] = new
         flipped_ref[:, span] = new.T
         half_ref[span, :] = new.astype(bf16).astype(f32)
     block = 64
-
-    def step(b, totals):
-        span = pl.ds(pl.multiple_of(b * block, block), block)
-        half = half_ref[span, :]
-        return [
-            totals[k]
-            + jnp.sum((projected_ref[k, span, :] * half).reshape(block // 8, 8, components), axis=0)
-            for k in range(trials)
-        ]
-
-    totals = lax.fori_loop(0, rows // block, step, [jnp.zeros((8, components), f32)] * trials, unroll=2)
+    totals = [jnp.zeros((8, components), f32)] * trials
+    for side, projected_ref in enumerate((near_ref, far_ref)):
+
+        def step(b, totals):
+            span = pl.ds(pl.multiple_of(b * block, block), block)
+            half = half_ref[pl.ds(pl.multiple_of(side * rows + b * block, block), block), :]
+            return [
+                totals[k]
+                + jnp.sum((projected_ref[k, span, :] * half).reshape(block // 8, 8, components), axis=0)
+                for k in range(trials)
+            ]
+
+        totals = lax.fori_loop(0, rows // block, step, totals, unroll=2)
     part = jnp.concatenate([jnp.sum(total, axis=0, keepdims=True) for total in totals], axis=0)
     for d in range(part_ref.shape[0]):
         part_ref[d, 0:trials, :] = part
         part_ref[d, trials:, :] = sent
 
 
-def trial_sum(gathered_ref, kept_ref, sum_ref):
+def trial_sum(gathered_ref, *refs):
+    sum_ref = refs[-1]
     tri = lax.axis_size("tri")
     chips = gathered_ref.shape[0]
     trials = gathered_ref.shape[1] - PAD
@@ -240,7 +257,7 @@
         sum_ref[t * trials : (t + 1) * trials, :] = total
 
 
-def second_system(count, gram_time_ref, gathered_ref, kept_ref, inverse_ref, gram_ref, *work):
+def second_system(count, gram_time_ref, gathered_ref, kept_ref, held_ref, inverse_ref, gram_ref, *work):
     components = gram_ref.shape[0]
     chips = gathered_ref.shape[0]
     trials = gathered_ref.shape[1] - PAD
@@ -257,20 +274,30 @@
 
 
 def time_pass(
-    ours_ref, theirs_ref, inverse_ref, flipped_ref, spikes_ref, new_ref,
+    ours_ref, theirs_ref, inverse_ref, flipped_ref, near_ref, far_ref, new_ref,
     new_hbm, trial_hbm, table_hbm, part_ref, table_ref, sems,
 ):
-    new_copy = pltpu.make_async_copy(new_ref, new_hbm, sems.at[0])
-    new_copy.start()
-    trials, rows, bins = spikes_ref.shape
+    trials, rows, bins = near_ref.shape
+    tri = lax.axis_size("tri")
+    half = lax.axis_index("tri") // (tri // 2)
+    moves = [
+        pltpu.make_async_copy(
+            new_ref.at[side * rows : (side + 1) * rows, :],
+            new_hbm.at[pl.ds(pl.multiple_of(lax.rem(half + side, 2) * rows, rows), rows), :],
+            sems.at[2 + side],
+        )
+        for side in range(2)
+    ]
+    for move in moves:
+        move.start()
     components = inverse_ref.shape[0]
     raw = dot(ours_ref[...] + theirs_ref[...], inverse_ref[...])
     scale = jnp.sqrt(jnp.sum(raw * raw, axis=0, keepdims=True) / raw.shape[0] + 1e-06)
     table_ref[...] = raw / scale
     span = pl.ds(pl.multiple_of(lax.axis_index("tri") * trials, trials), trials)
     copies = [
-        pltpu.make_async_copy(table_ref.at[span, :], trial_hbm, sems.at[1]),
-        pltpu.make_async_copy(table_ref, table_hbm, sems.at[2]),
+        pltpu.make_async_copy(table_ref.at[span, :], trial_hbm, sems.at[0]),
+        pltpu.make_async_copy(table_ref, table_hbm, sems.at[1]),
     ]
     for copy in copies:
         copy.start()
@@ -278,10 +305,12 @@
     total = None
     for k in range(trials):
         khatri_rao = (flipped_ref[...] * columns[:, k : k + 1]).astype(bf16)
-        term = jnp.dot(khatri_rao, spikes_ref[k], preferred_element_type=f32)
-        total = term if total is None else total + term
+        for side, spikes_ref in enumerate((near_ref, far_ref)):
+            piece = khatri_rao[:, side * rows : (side + 1) * rows]
+            term = jnp.dot(piece, spikes_ref[k], preferred_element_type=f32)
+            total = term if total is None else total + term
     part_ref[...] = total
-    for copy in [new_copy] + copies:
+    for copy in moves + copies:
         copy.wait()
 
 
@@ -311,35 +340,49 @@
     square = array(components, components)
     work = [pltpu.VMEM((components, components), f32)] * 3
 
-    spikes, projected, part = call(
-        neuron_pass,
-        [
-            pltpu.VMEM(spike_counts.shape, bf16),
-            pltpu.VMEM((trials, rows, components), f32),
-            array(tri, block + trials, components),
-        ],
-        "neuron_pass",
-        [in_hbm] * 3,
-        LIM1,
-        [
-            pltpu.VMEM(time_factor.shape, bf16),
-            pltpu.VMEM((trials, components), bf16),
-            pltpu.SemaphoreType.DMA((tri + 2,)),
-        ],
-    )(spike_counts, *[pltpu.with_memory_space_constraint(a, pltpu.HBM) for a in (time_factor, trial_factor)])
-    parts = lax.all_to_all(part, "tri", 0, 0)
+    rings = [list(range(x * ring, (x + 1) * ring)) for x in range(2)]
+    fetched = [pltpu.with_memory_space_constraint(a, pltpu.HBM) for a in (spike_counts, time_factor, trial_factor)]
+
+    def first_pass(far, parts, *before):
+        return call(
+            lambda *refs: neuron_pass(far, *refs),
+            [
+                pltpu.VMEM((trials, rows // 2, bins), bf16),
+                pltpu.VMEM((trials, rows // 2, components), f32),
+            ]
+            + parts,
+            "far_pass" if far else "near_pass",
+            [in_hbm] * 3 + [WHOLE] * len(before),
+            LIM1,
+            [
+                pltpu.VMEM(time_factor.shape, bf16),
+                pltpu.VMEM((trials, components), bf16),
+                pltpu.SemaphoreType.DMA((ring + 2,)),
+            ],
+        )(*fetched, *before)
+
+    def pass_on(value, x, z):
+        pairs = [(t, (t // ring + x) % 2 * ring + (t % ring + z) % ring) for t in range(tri)]
+        return lax.ppermute(value, "tri", pairs)
+
+    pieces = [array(block + trials, components)] * ring
+    spikes_far, projected_far, *far = first_pass(True, pieces)
+    received = [pass_on(far[k], 1, k) for k in range(ring)]
+    spikes_near, projected_near, *near = first_pass(False, pieces, held(spikes_far), held(projected_far))
+    received += [near[0]] + [pass_on(near[k], 0, k) for k in range(1, ring)]
+    spikes = [held(spikes_near), held(spikes_far)]
+    projected = [held(projected_near), held(projected_far)]
     copies, gram_time = call(
         neuron_solve,
         [array(ring, block, components), square],
         "neuron_solve",
-        [WHOLE] * 4,
+        [WHOLE] * (tri + 5),
         5,
         [pltpu.VMEM((tri * trials, components), bf16)] + work,
-    )(parts, time_factor, held(projected), held(spikes))
-    rings = [list(range(x * ring, (x + 1) * ring)) for x in range(2)]
+    )(*received, time_factor, *projected, *spikes)
     near = lax.all_to_all(copies, "tri", 0, 0, axis_index_groups=rings).reshape(rows // 2, components)
     far = lax.ppermute(near, "tri", [(t, (t + ring) % tri) for t in range(tri)])
-    (gram_part,) = call(neuron_gram, [square], "neuron_gram", [WHOLE] * 3)(near, held(projected), held(spikes))
+    (gram_part,) = call(neuron_gram, [square], "neuron_gram", [WHOLE] * 5)(near, *projected, *spikes)
     (packed,) = call(
         pack_gram, [array(neu, components // neu + PAD, components)], "pack_gram", [WHOLE] * 2
     )(gram_part, lax.ppermute(gram_part, "neu", swap))
@@ -355,17 +398,17 @@
             array(half * tri, trials + PAD, components),
         ],
         "trial_pass",
-        [WHOLE] * 5,
+        [WHOLE] * 7,
         5,
         [pltpu.VMEM((rows, components), f32)],
-    )(grams, near, far, held(projected), held(spikes))
+    )(grams, near, far, *projected, *spikes)
     groups = [[n * tri + t for n in range(c, neu, 2) for t in range(tri)] for c in range(2)]
     gathered = lax.all_to_all(trial_part, both, 0, 0, axis_index_groups=groups)
-    (ours,) = call(trial_sum, [array(tri * trials, components)], "trial_sum", [WHOLE] * 2)(gathered, held(spikes))
+    (ours,) = call(trial_sum, [array(tri * trials, components)], "trial_sum", [WHOLE] * 3)(gathered, *spikes)
     theirs = lax.ppermute(ours, "neu", swap)
     inverse_two, gram_neuron = call(
-        lambda *refs: second_system(neu * rows, *refs), [square, square], "second_system", [WHOLE] * 3, 4, work
-    )(gram_time, gathered, held(spikes))
+        lambda *refs: second_system(neu * rows, *refs), [square, square], "second_system", [WHOLE] * 4, 4, work
+    )(gram_time, gathered, *spikes)
     neuron_new, trial_new, trial_table, time_part = call(
         time_pass,
         [
@@ -375,14 +418,14 @@
             array(components, bins),
         ],
         "time_pass",
-        [WHOLE] * 6,
+        [WHOLE] * 7,
         5,
         [
             pltpu.VMEM((tri * trials, components), f32),
-            pltpu.SemaphoreType.DMA((3,)),
+            pltpu.SemaphoreType.DMA((4,)),
         ],
         [in_hbm] * 3 + [WHOLE],
-    )(ours, theirs, inverse_two, flipped, held(spikes), held(new))
+    )(ours, theirs, inverse_two, flipped, *spikes, held(new))
     pieces = lax.all_to_all(time_part.reshape(neu * tri, components // (neu * tri), bins), both, 0, 0)
     (inverse_three,) = call(third_system, [square], "third_system", [WHOLE] * 2, 4, work)(gram_neuron, trial_table)
     piece = jnp.sum(pieces, axis=0, keepdims=True)

time: 120 us -> 119 us (level)
  blocking collectives: 75.9 us -> 57.9 us
  starting transfers between devices: 11.7 us -> 23.4 us
  waiting for transfers between devices: 6.63 us -> 11.7 us
    all_to_all x1 -> x0, blocking collectives: 21.9 us -> none  [body(): parts = lax.all_to_all(part, 'tri', 0, 0)]
    ppermute x0 -> x7, starting transfers between devices: none -> 12 us  [pass_on(): return lax.ppermute(value, 'tri', pairs)]
    ppermute x0 -> x7, waiting for transfers between devices: none -> 4.64 us  [pass_on(): return lax.ppermute(value, 'tri', pairs)]
    all_to_all x1, blocking collectives: 9.36 us -> 13.2 us  [body(): lax.all_to_all(copies, 'tri', 0, 0, axis_index_groups=rings)]
    pallas_call x3 -> x4, Pallas kernels: 7.72 us -> 9.39 us  [the longest x2 9.02 us: first_pass(): call(lambda *refs: neuron_pass(far, *refs), [pltpu.VMEM((trials, rows //...]
  transfers between devices with their start and end apart: 4 -> 11, of which waited for: 2 -> 5; matrix products, arithmetic and copies ran while one was open for 0% -> 0% of each run, Pallas kernels for 6% -> 10%
where the time goes in v6:
time: 119 us
  blocking collectives  57.9 us (49%)
  Pallas kernels  24.1 us (20%)
  starting transfers between devices  23.4 us (20%)
  waiting for transfers between devices  11.7 us (10%)
    all_to_all x1, blocking collectives, body(): gathered = lax.all_to_all(trial_part, both, 0, 0, axis_index_groups=groups)  17.9 us
    all_to_all x1, blocking collectives, body(): grams = lax.all_to_all(packed, both, 0, 0, axis_index_groups=groups)  13.8 us
    all_to_all x1, blocking collectives, body(): lax.all_to_all(copies, 'tri', 0, 0, axis_index_groups=rings)  13.2 us
    all_to_all x1, blocking collectives, body(): lax.all_to_all(time_part.reshape(neu * tri, components // (neu * tri), bi...  13 us
    ppermute x7, starting transfers between devices, pass_on(): return lax.ppermute(value, 'tri', pairs)  12 us
    pallas_call x2, Pallas kernels, first_pass(): call(lambda *refs: neuron_pass(far, *refs), [pltpu.VMEM((trials, rows //...  9.02 us
    all_to_all x1, waiting for transfers between devices, body(): lax.all_to_all(jnp.broadcast_to(piece, pieces.shape), both, 0, 0)  6.11 us
    ppermute x7, waiting for transfers between devices, pass_on(): return lax.ppermute(value, 'tri', pairs)  4.64 us
  transfers between devices with their start and end apart: 11, of which 5 were waited for; matrix products, arithmetic and copies ran while one was open for 0% of the time, Pallas kernels for 10%

profile of v6, /device:TPU:1, one launch (start us, length us, event | category | flops | bytes accessed | tf_op | source)
XLA Modules:
  0.0 118.7 jit_solution(414898304673663928)
XLA Ops:
  0.6 4.5 %far_pass.1 = (bf16[16,1024,256]{2,1,0:T(8,128)(2,1)S(1)}, f32[16,1024,128]{2,1,0:T(8,128)S(1)}, f32[272,128]{1,0:T(8,128)S(1)}, f32[272,128]{1,0:T(8,128)S(1)},...) custom-call(bf16[16,2048,256]{2,1,0:T(8,128)(2,1)} %refs_0_.3, bf16[256,128]{1,0:T(8,128)(2,1)} %refs_8_.1, ...), custom_call_target="tpu_custom_call" | custom-call | tf_op jit(solution)/shard_map/far_pass/pallas_call | solution.py:347
  5.1 2.1 %collective-permute-start = (f32[272,128]{1,0:T(8,128)S(1)}, f32[272,128]{1,0:T(8,128)S(1)}, u32[]{:S(2)}, u32[]{:S(2)}) collective-permute-start(f32[272,128]{1,0:T(8,128)S(1)} %get-tuple-element.29), channel_id=1, source_target_pairs={{0,4},{1,5},{2,6},{3,7},{4,0},{5,1},{6,2},{7,3},{8,12},{9,13},{10,... | collective-permute-start | bytes 417800 | tf_op jit(solution)/shard_map/ppermute | solution.py:366
  7.3 1.6 %collective-permute-start.1 = (f32[272,128]{1,0:T(8,128)S(1)}, f32[272,128]{1,0:T(8,128)S(1)}, u32[]{:S(2)}, u32[]{:S(2)}) collective-permute-start(f32[272,128]{1,0:T(8,128)S(1)} %get-tuple-element.30), channel_id=1, source_target_pairs={{0,5},{1,6},{2,7},{3,4},{4,1},{5,2},{6,3},{7,0},{8,13},{9,14},{10,... | collective-permute-start | bytes 417800 | tf_op jit(solution)/shard_map/ppermute | solution.py:366
  8.9 4.2 %collective-permute-start.2 = (f32[272,128]{1,0:T(8,128)S(1)}, f32[272,128]{1,0:T(8,128)S(1)}, u32[]{:S(2)}, u32[]{:S(2)}) collective-permute-start(f32[272,128]{1,0:T(8,128)S(1)} %get-tuple-element.31), channel_id=1, source_target_pairs={{0,6},{1,7},{2,4},{3,5},{4,2},{5,3},{6,0},{7,1},{8,14},{9,15},{10,... | collective-permute-start | bytes 417800 | tf_op jit(solution)/shard_map/ppermute | solution.py:366
  13.1 0.7 collective-permute-start.3
  13.8 0.0 copy-start
  13.8 4.5 %near_pass.1 = (bf16[16,1024,256]{2,1,0:T(8,128)(2,1)S(1)}, f32[16,1024,128]{2,1,0:T(8,128)S(1)}, f32[272,128]{1,0:T(8,128)S(1)}, f32[272,128]{1,0:T(8,128)S(1)}...) custom-call(bf16[16,2048,256]{2,1,0:T(8,128)(2,1)} %refs_0_.3, bf16[256,128]{1,0:T(8,128)(2,1)} %refs_8_.1, ...), custom_call_target="tpu_custom_call" | custom-call | tf_op jit(solution)/shard_map/near_pass/pallas_call | solution.py:347
  18.3 0.8 collective-permute-start.4
  19.1 0.0 collective-permute-done.refs_0_
  19.1 0.5 collective-permute-start.5
  19.6 0.0 collective-permute-done.1.refs_1_
  19.6 2.0 %collective-permute-start.6 = (f32[272,128]{1,0:T(8,128)S(1)}, f32[272,128]{1,0:T(8,128)S(1)}, u32[]{:S(2)}, u32[]{:S(2)}) collective-permute-start(f32[272,128]{1,0:T(8,128)S(1)} %get-tuple-element.38), channel_id=1, source_target_pairs={{0,3},{1,0},{2,1},{3,2},{4,7},{5,4},{6,5},{7,6},{8,11},{9,8},{10,9... | collective-permute-start | bytes 417800 | tf_op jit(solution)/shard_map/ppermute | solution.py:366
  21.6 0.0 collective-permute-done.2.refs_2_
  21.6 0.0 collective-permute-done.3.refs_3_
  21.6 2.4 %collective-permute-done.4.refs_5_ = f32[272,128]{1,0:T(8,128)S(1)} collective-permute-done((f32[272,128]{1,0:T(8,128)S(1)}, f32[272,128]{1,0:T(8,128)S(1)}, u32[]{:S(2)}, u32[]{:S(2)}) %collective-permute-start.4) | collective-permute-done | bytes 139296 | tf_op jit(solution)/shard_map/ppermute | solution.py:366
  24.0 1.5 %collective-permute-done.5.refs_6_ = f32[272,128]{1,0:T(8,128)S(1)} collective-permute-done((f32[272,128]{1,0:T(8,128)S(1)}, f32[272,128]{1,0:T(8,128)S(1)}, u32[]{:S(2)}, u32[]{:S(2)}) %collective-permute-start.5) | collective-permute-done | bytes 139296 | tf_op jit(solution)/shard_map/ppermute | solution.py:366
  25.6 0.7 collective-permute-done.6.refs_7_
  26.3 0.0 copy-done
  26.3 2.7 %neuron_solve.1 = (f32[4,256,128]{2,1,0:T(8,128)S(1)}, f32[128,128]{1,0:T(8,128)S(1)}) custom-call(f32[272,128]{1,0:T(8,128)S(1)} %collective-permute-done.refs_0_, f32[272,128]{1,0:T(8,128)S(1)} %collective-permute-done.1.refs_1_, f32[272,128]{1,0:T(8,128)S(1)} %collective-permute-done.2.refs_2_, f32[272,128]{1,0:T(8,128)S(1)} %collective-permute-done.3.refs_3_, ...), custom_call_target="tpu_custom_call" | custom-call | tf_op jit(solution)/shard_map/neuron_solve/pallas_call | solution.py:375
  28.9 13.2 %all_to_all.25 = f32[4,256,128]{2,1,0:T(8,128)S(1)} all-to-all(f32[4,256,128]{2,1,0:T(8,128)S(1)} %get-tuple-element.41), channel_id=1, replica_groups={{0,1,2,3},{4,5,6,7},{8,9,10,11},{12,13,14,15},{16,17,18,19},{20,21,22,2..., dimensions={0} | all-to-all | bytes 1048576 | tf_op jit(solution)/shard_map/all_to_all | solution.py:383
  42.1 1.0 collective-permute-start.8
  43.1 0.3 neuron_gram.1.ours_ref
  43.4 3.0 %collective-permute-start.7 = (f32[128,128]{1,0:T(8,128)S(1)}, f32[128,128]{1,0:T(8,128)S(1)}, u32[]{:S(2)}, u32[]{:S(2)}) collective-permute-start(f32[128,128]{1,0:T(8,128)S(1)} %neuron_gram.1.ours_ref), channel_id=1, source_target_pairs={{0,8},{8,0},{16,24},{24,16},{32,40},{40,32},{48,56},{56,48},{64,72... | collective-permute-start | bytes 196616 | tf_op jit(solution)/shard_map/ppermute | solution.py:388
  46.4 0.9 collective-permute-done.7.theirs_ref
  47.3 13.8 %all_to_all.26.refs_0_ = f32[16,16,128]{2,1,0:T(8,128)S(1)} all-to-all(f32[16,16,128]{2,1,0:T(8,128)S(1)} %pack_gram.1), channel_id=1, replica_groups={{0,4,16,20,32,36,48,52,64,68,80,84,96,100,112,116},{1,5,17,21,33,37,49,..., dimensions={0} | all-to-all | bytes 262144 | tf_op jit(solution)/shard_map/all_to_all | solution.py:392
  61.1 0.0 collective-permute-done.8.refs_2_
  61.1 1.6 %trial_pass.1 = (f32[2048,128]{1,0:T(8,128)S(1)}, f32[128,2048]{1,0:T(8,128)S(1)}, f32[64,24,128]{2,1,0:T(8,128)S(1)}) custom-call(f32[16,16,128]{2,1,0:T(8,128)S(1)} %all_to_all.26.refs_0_, f32[1024,128]{1,0:T(8,128)S(1)} %bitcast.8, f32[1024,128]{1,0:T(8,128)S(1)} %collective-permute-done.8.refs_2_, ...), custom_call_target="tpu_custom_call" | custom-call | tf_op jit(solution)/shard_map/trial_pass/pallas_call | solution.py:393
  62.8 17.9 %all_to_all.27.gathered_ref.refs_1_ = f32[64,24,128]{2,1,0:T(8,128)S(1)} all-to-all(f32[64,24,128]{2,1,0:T(8,128)S(1)} %get-tuple-element.42), channel_id=1, replica_groups={{0,1,2,3,4,5,6,7,16,17,18,19,20,21,22,23,32,33,34,35,36,37,38,39,48,49,..., dimensions={0} | all-to-all | bytes 1572864 | tf_op jit(solution)/shard_map/all_to_all | solution.py:406
  80.7 3.2 %collective-permute-start.9 = (f32[128,128]{1,0:T(8,128)S(1)}, f32[128,128]{1,0:T(8,128)S(1)}, u32[]{:S(2)}, u32[]{:S(2)}) collective-permute-start(f32[128,128]{1,0:T(8,128)S(1)} %trial_sum.1.ours_ref), channel_id=1, source_target_pairs={{0,8},{8,0},{16,24},{24,16},{32,40},{40,32},{48,56},{56,48},{64,72... | collective-permute-start | bytes 196616 | tf_op jit(solution)/shard_map/ppermute | solution.py:408
  83.9 2.5 %second_system.1 = (f32[128,128]{1,0:T(8,128)S(1)}, f32[128,128]{1,0:T(8,128)S(1)}) custom-call(f32[128,128]{1,0:T(8,128)S(1)} %get-tuple-element.43.refs_0_, f32[64,24,128]{2,1,0:T(8,128)S(1)} %all_to_all.27.gathered_ref.refs_1_, bf16[16,1024,256]{2,1,0:T(8,128)(2,1)S(1)} %get-tuple-element.40.refs_11_.refs_2_.refs_5_.refs_0_.near_ref, ...), custom_call_target="tpu_custom_call" | custom-call | tf_op jit(solution)/shard_map/second_system/pallas_call | solution.py:409
  86.4 0.0 collective-permute-done.9.theirs_ref
  86.4 2.9 %time_pass.1 = (f32[2048,128]{1,0:T(8,128)}, f32[16,128]{1,0:T(8,128)}, f32[128,128]{1,0:T(8,128)S(1)}, f32[128,256]{1,0:T(8,128)S(1)}) custom-call(f32[128,128]{1,0:T(8,128)S(1)} %trial_sum.1.ours_ref, f32[128,128]{1,0:T(8,128)S(1)} %collective-permute-done.9.theirs_ref, f32[128,128]{1,0:T(8,128)S(1)} %get-tuple-element.44.inverse_ref, ...), custom_call_target="tpu_custom_call" | custom-call | tf_op jit(solution)/shard_map/time_pass/pallas_call | solution.py:412
  89.3 0.1 copy.7
  89.4 13.0 %all_to_all.28 = f32[128,1,256]{2,1,0:T(1,128)S(1)} all-to-all(f32[128,1,256]{2,1,0:T(1,128)S(1)} %copy.7), channel_id=1, replica_groups=mesh['neu'=16,'tri'=8] {'neu','tri'}, dimensions={0} | all-to-all | bytes 262144 | tf_op jit(solution)/shard_map/all_to_all | solution.py:429
  102.5 0.2 reduce_sum.9
  102.6 0.7 broadcast_in_dim.2
  103.3 4.3 %all-to-all-start.4 = ((f32[128,1,256]{2,1,0:T(1,128)}), f32[128,1,256]{2,1,0:T(1,128)S(1)}, u32[]{:S(2)}, u32[]{:S(2)}) async-start(f32[128,1,256]{2,1,0:T(1,128)} %broadcast_in_dim.2), calls=%async_computation.4 | async-start | bytes 262144 | tf_op jit(solution)/shard_map/all_to_all | solution.py:432
  107.6 4.0 %third_system.1.inverse_ref = f32[128,128]{1,0:T(8,128)S(1)} custom-call(f32[128,128]{1,0:T(8,128)S(1)} %get-tuple-element.50.gram_neuron_ref, f32[128,128]{1,0:T(8,128)S(1)} %get-tuple-element.51.table_ref), custom_call_target="tpu_custom_call" | custom-call | tf_op jit(solution)/shard_map/third_system/pallas_call | solution.py:430
  111.6 6.1 %all-to-all-done.4 = f32[128,1,256]{2,1,0:T(1,128)S(1)} async-done(((f32[128,1,256]{2,1,0:T(1,128)}), f32[128,1,256]{2,1,0:T(1,128)S(1)}, u32[]{:S(2)}, u32[]{:S(2)}) %all-to-all-start.4) | async-done | bytes 131104 | tf_op jit(solution)/shard_map/all_to_all | solution.py:432
  117.7 1.0 time_solve.1
  (3 shorter events, 0.1 us)
Async XLA Ops:
  5.1 14.0 %collective-permute-start = (f32[272,128]{1,0:T(8,128)S(1)}, f32[272,128]{1,0:T(8,128)S(1)}, u32[]{:S(2)}, u32[]{:S(2)}) collective-permute-start(f32[272,128]{1,0:T(8,128)S(1)} %get-tuple-element.29), channel_id=1, source_target_pairs={{0,4},{1,5},{2,6},{3,7},{4,0},{5,1},{6,2},{7,3},{8,12},{9,13},{10,... | collective-permute-start | bytes 417800 | tf_op jit(solution)/shard_map/ppermute | solution.py:366
  7.3 12.4 %collective-permute-start.1 = (f32[272,128]{1,0:T(8,128)S(1)}, f32[272,128]{1,0:T(8,128)S(1)}, u32[]{:S(2)}, u32[]{:S(2)}) collective-permute-start(f32[272,128]{1,0:T(8,128)S(1)} %get-tuple-element.30), channel_id=1, source_target_pairs={{0,5},{1,6},{2,7},{3,4},{4,1},{5,2},{6,3},{7,0},{8,13},{9,14},{10,... | collective-permute-start | bytes 417800 | tf_op jit(solution)/shard_map/ppermute | solution.py:366
  8.9 12.8 %collective-permute-start.2 = (f32[272,128]{1,0:T(8,128)S(1)}, f32[272,128]{1,0:T(8,128)S(1)}, u32[]{:S(2)}, u32[]{:S(2)}) collective-permute-start(f32[272,128]{1,0:T(8,128)S(1)} %get-tuple-element.31), channel_id=1, source_target_pairs={{0,6},{1,7},{2,4},{3,5},{4,2},{5,3},{6,0},{7,1},{8,14},{9,15},{10,... | collective-permute-start | bytes 417800 | tf_op jit(solution)/shard_map/ppermute | solution.py:366
  13.1 8.5 %collective-permute-start.3 = (f32[272,128]{1,0:T(8,128)S(1)}, f32[272,128]{1,0:T(8,128)S(1)}, u32[]{:S(2)}, u32[]{:S(2)}) collective-permute-start(f32[272,128]{1,0:T(8,128)S(1)} %get-tuple-element.32), channel_id=1, source_target_pairs={{0,7},{1,4},{2,5},{3,6},{4,3},{5,0},{6,1},{7,2},{8,15},{9,12},{10,... | collective-permute-start | bytes 417800 | tf_op jit(solution)/shard_map/ppermute | solution.py:366
  13.8 12.5 %copy-start = (bf16[256,128]{1,0:T(8,128)(2,1)S(1)}, bf16[256,128]{1,0:T(8,128)(2,1)}, u32[]{:S(2)}) copy-start(bf16[256,128]{1,0:T(8,128)(2,1)} %refs_8_.1) | copy-start | bytes 196612
  18.3 5.7 %collective-permute-start.4 = (f32[272,128]{1,0:T(8,128)S(1)}, f32[272,128]{1,0:T(8,128)S(1)}, u32[]{:S(2)}, u32[]{:S(2)}) collective-permute-start(f32[272,128]{1,0:T(8,128)S(1)} %get-tuple-element.36), channel_id=1, source_target_pairs={{0,1},{1,2},{2,3},{3,0},{4,5},{5,6},{6,7},{7,4},{8,9},{9,10},{10,1... | collective-permute-start | bytes 417800 | tf_op jit(solution)/shard_map/ppermute | solution.py:366
  19.1 6.4 %collective-permute-start.5 = (f32[272,128]{1,0:T(8,128)S(1)}, f32[272,128]{1,0:T(8,128)S(1)}, u32[]{:S(2)}, u32[]{:S(2)}) collective-permute-start(f32[272,128]{1,0:T(8,128)S(1)} %get-tuple-element.37), channel_id=1, source_target_pairs={{0,2},{1,3},{2,0},{3,1},{4,6},{5,7},{6,4},{7,5},{8,10},{9,11},{10,... | collective-permute-start | bytes 417800 | tf_op jit(solution)/shard_map/ppermute | solution.py:366
  19.6 6.6 %collective-permute-start.6 = (f32[272,128]{1,0:T(8,128)S(1)}, f32[272,128]{1,0:T(8,128)S(1)}, u32[]{:S(2)}, u32[]{:S(2)}) collective-permute-start(f32[272,128]{1,0:T(8,128)S(1)} %get-tuple-element.38), channel_id=1, source_target_pairs={{0,3},{1,0},{2,1},{3,2},{4,7},{5,4},{6,5},{7,6},{8,11},{9,8},{10,9... | collective-permute-start | bytes 417800 | tf_op jit(solution)/shard_map/ppermute | solution.py:366
  42.1 19.0 %collective-permute-start.8 = (f32[1024,128]{1,0:T(8,128)S(1)}, f32[1024,128]{1,0:T(8,128)S(1)}, u32[]{:S(2)}, u32[]{:S(2)}) collective-permute-start(f32[1024,128]{1,0:T(8,128)S(1)} %bitcast.6), channel_id=1, source_target_pairs={{0,4},{1,5},{2,6},{3,7},{4,0},{5,1},{6,2},{7,3},{8,12},{9,13},{10,... | collective-permute-start | bytes 1572872 | tf_op jit(solution)/shard_map/ppermute | solution.py:384
  43.4 3.9 %collective-permute-start.7 = (f32[128,128]{1,0:T(8,128)S(1)}, f32[128,128]{1,0:T(8,128)S(1)}, u32[]{:S(2)}, u32[]{:S(2)}) collective-permute-start(f32[128,128]{1,0:T(8,128)S(1)} %neuron_gram.1.ours_ref), channel_id=1, source_target_pairs={{0,8},{8,0},{16,24},{24,16},{32,40},{40,32},{48,56},{56,48},{64,72... | collective-permute-start | bytes 196616 | tf_op jit(solution)/shard_map/ppermute | solution.py:388
  80.7 5.7 %collective-permute-start.9 = (f32[128,128]{1,0:T(8,128)S(1)}, f32[128,128]{1,0:T(8,128)S(1)}, u32[]{:S(2)}, u32[]{:S(2)}) collective-permute-start(f32[128,128]{1,0:T(8,128)S(1)} %trial_sum.1.ours_ref), channel_id=1, source_target_pairs={{0,8},{8,0},{16,24},{24,16},{32,40},{40,32},{48,56},{56,48},{64,72... | collective-permute-start | bytes 196616 | tf_op jit(solution)/shard_map/ppermute | solution.py:408
  103.3 14.3 %all-to-all-start.4 = ((f32[128,1,256]{2,1,0:T(1,128)}), f32[128,1,256]{2,1,0:T(1,128)S(1)}, u32[]{:S(2)}, u32[]{:S(2)}) async-start(f32[128,1,256]{2,1,0:T(1,128)} %broadcast_in_dim.2), calls=%async_computation.4 | async-start | bytes 262144 | tf_op jit(solution)/shard_map/all_to_all | solution.py:432

commit v7 on v6

--- a/solution.py
+++ b/solution.py
@@ -11,7 +11,7 @@
 highest = lax.Precision.HIGHEST
 WHOLE = pl.BlockSpec(memory_space=pltpu.VMEM)
 MIB = 1 << 20
-AHEAD = 3
+AHEAD = 4
 PAD = 8
 
 
@@ -320,7 +320,7 @@
 
 
 def time_solve(mttkrp_ref, inverse_ref, time_ref, weights_ref):
-    raw = dot(inverse_ref[...], mttkrp_ref[...]).T
+    raw = fine(inverse_ref[...], mttkrp_ref[...]).T
     weights = jnp.sqrt(jnp.mean(raw * raw, axis=0, keepdims=True) + 1e-06)
     weights_ref[...] = weights
     time_ref[...] = raw / weights

time: 119 us -> 120 us (level)
  no operation moved by 1% of the time
where the time goes in v7:
time: 120 us; the launch traced here: 119 us
  blocking collectives  57.9 us (48%)
  Pallas kernels  25.2 us (21%)
  starting transfers between devices  23.4 us (20%)
  waiting for transfers between devices  11.3 us (9%)
    all_to_all x1, blocking collectives, body(): gathered = lax.all_to_all(trial_part, both, 0, 0, axis_index_groups=groups)  17.9 us
    all_to_all x1, blocking collectives, body(): grams = lax.all_to_all(packed, both, 0, 0, axis_index_groups=groups)  13.8 us
    all_to_all x1, blocking collectives, body(): lax.all_to_all(copies, 'tri', 0, 0, axis_index_groups=rings)  13.2 us
    all_to_all x1, blocking collectives, body(): lax.all_to_all(time_part.reshape(neu * tri, components // (neu * tri), bi...  13 us
    ppermute x7, starting transfers between devices, pass_on(): return lax.ppermute(value, 'tri', pairs)  12 us
    pallas_call x2, Pallas kernels, first_pass(): call(lambda *refs: neuron_pass(far, *refs), [pltpu.VMEM((trials, rows //...  9.02 us
    all_to_all x1, waiting for transfers between devices, body(): lax.all_to_all(jnp.broadcast_to(piece, pieces.shape), both, 0, 0)  5.71 us
    ppermute x7, waiting for transfers between devices, pass_on(): return lax.ppermute(value, 'tri', pairs)  4.64 us
  transfers between devices with their start and end apart: 11, of which 5 were waited for; matrix products, arithmetic and copies ran while one was open for 0% of the time, Pallas kernels for 10%

profile of v7, /device:TPU:1, one launch (start us, length us, event | category | flops | bytes accessed | tf_op | source)
XLA Modules:
  0.0 119.5 jit_solution(6606120954975481302)
XLA Ops:
  0.6 4.5 %far_pass.1 = (bf16[16,1024,256]{2,1,0:T(8,128)(2,1)S(1)}, f32[16,1024,128]{2,1,0:T(8,128)S(1)}, f32[272,128]{1,0:T(8,128)S(1)}, f32[272,128]{1,0:T(8,128)S(1)},...) custom-call(bf16[16,2048,256]{2,1,0:T(8,128)(2,1)} %refs_0_.3, bf16[256,128]{1,0:T(8,128)(2,1)} %refs_8_.1, ...), custom_call_target="tpu_custom_call" | custom-call | tf_op jit(solution)/shard_map/far_pass/pallas_call | solution.py:347
  5.1 2.1 %collective-permute-start = (f32[272,128]{1,0:T(8,128)S(1)}, f32[272,128]{1,0:T(8,128)S(1)}, u32[]{:S(2)}, u32[]{:S(2)}) collective-permute-start(f32[272,128]{1,0:T(8,128)S(1)} %get-tuple-element.29), channel_id=1, source_target_pairs={{0,4},{1,5},{2,6},{3,7},{4,0},{5,1},{6,2},{7,3},{8,12},{9,13},{10,... | collective-permute-start | bytes 417800 | tf_op jit(solution)/shard_map/ppermute | solution.py:366
  7.3 1.6 %collective-permute-start.1 = (f32[272,128]{1,0:T(8,128)S(1)}, f32[272,128]{1,0:T(8,128)S(1)}, u32[]{:S(2)}, u32[]{:S(2)}) collective-permute-start(f32[272,128]{1,0:T(8,128)S(1)} %get-tuple-element.30), channel_id=1, source_target_pairs={{0,5},{1,6},{2,7},{3,4},{4,1},{5,2},{6,3},{7,0},{8,13},{9,14},{10,... | collective-permute-start | bytes 417800 | tf_op jit(solution)/shard_map/ppermute | solution.py:366
  8.9 4.2 %collective-permute-start.2 = (f32[272,128]{1,0:T(8,128)S(1)}, f32[272,128]{1,0:T(8,128)S(1)}, u32[]{:S(2)}, u32[]{:S(2)}) collective-permute-start(f32[272,128]{1,0:T(8,128)S(1)} %get-tuple-element.31), channel_id=1, source_target_pairs={{0,6},{1,7},{2,4},{3,5},{4,2},{5,3},{6,0},{7,1},{8,14},{9,15},{10,... | collective-permute-start | bytes 417800 | tf_op jit(solution)/shard_map/ppermute | solution.py:366
  13.1 0.7 collective-permute-start.3
  13.8 0.0 copy-start
  13.8 4.5 %near_pass.1 = (bf16[16,1024,256]{2,1,0:T(8,128)(2,1)S(1)}, f32[16,1024,128]{2,1,0:T(8,128)S(1)}, f32[272,128]{1,0:T(8,128)S(1)}, f32[272,128]{1,0:T(8,128)S(1)}...) custom-call(bf16[16,2048,256]{2,1,0:T(8,128)(2,1)} %refs_0_.3, bf16[256,128]{1,0:T(8,128)(2,1)} %refs_8_.1, ...), custom_call_target="tpu_custom_call" | custom-call | tf_op jit(solution)/shard_map/near_pass/pallas_call | solution.py:347
  18.3 0.8 collective-permute-start.4
  19.1 0.0 collective-permute-done.refs_0_
  19.1 0.5 collective-permute-start.5
  19.6 0.0 collective-permute-done.1.refs_1_
  19.6 2.0 %collective-permute-start.6 = (f32[272,128]{1,0:T(8,128)S(1)}, f32[272,128]{1,0:T(8,128)S(1)}, u32[]{:S(2)}, u32[]{:S(2)}) collective-permute-start(f32[272,128]{1,0:T(8,128)S(1)} %get-tuple-element.38), channel_id=1, source_target_pairs={{0,3},{1,0},{2,1},{3,2},{4,7},{5,4},{6,5},{7,6},{8,11},{9,8},{10,9... | collective-permute-start | bytes 417800 | tf_op jit(solution)/shard_map/ppermute | solution.py:366
  21.6 0.0 collective-permute-done.2.refs_2_
  21.6 0.0 collective-permute-done.3.refs_3_
  21.6 2.4 %collective-permute-done.4.refs_5_ = f32[272,128]{1,0:T(8,128)S(1)} collective-permute-done((f32[272,128]{1,0:T(8,128)S(1)}, f32[272,128]{1,0:T(8,128)S(1)}, u32[]{:S(2)}, u32[]{:S(2)}) %collective-permute-start.4) | collective-permute-done | bytes 139296 | tf_op jit(solution)/shard_map/ppermute | solution.py:366
  24.0 1.5 %collective-permute-done.5.refs_6_ = f32[272,128]{1,0:T(8,128)S(1)} collective-permute-done((f32[272,128]{1,0:T(8,128)S(1)}, f32[272,128]{1,0:T(8,128)S(1)}, u32[]{:S(2)}, u32[]{:S(2)}) %collective-permute-start.5) | collective-permute-done | bytes 139296 | tf_op jit(solution)/shard_map/ppermute | solution.py:366
  25.6 0.7 collective-permute-done.6.refs_7_
  26.3 0.0 copy-done
  26.3 3.1 %neuron_solve.1 = (f32[4,256,128]{2,1,0:T(8,128)S(1)}, f32[128,128]{1,0:T(8,128)S(1)}) custom-call(f32[272,128]{1,0:T(8,128)S(1)} %collective-permute-done.refs_0_, f32[272,128]{1,0:T(8,128)S(1)} %collective-permute-done.1.refs_1_, f32[272,128]{1,0:T(8,128)S(1)} %collective-permute-done.2.refs_2_, f32[272,128]{1,0:T(8,128)S(1)} %collective-permute-done.3.refs_3_, ...), custom_call_target="tpu_custom_call" | custom-call | tf_op jit(solution)/shard_map/neuron_solve/pallas_call | solution.py:375
  29.3 13.2 %all_to_all.25 = f32[4,256,128]{2,1,0:T(8,128)S(1)} all-to-all(f32[4,256,128]{2,1,0:T(8,128)S(1)} %get-tuple-element.41), channel_id=1, replica_groups={{0,1,2,3},{4,5,6,7},{8,9,10,11},{12,13,14,15},{16,17,18,19},{20,21,22,2..., dimensions={0} | all-to-all | bytes 1048576 | tf_op jit(solution)/shard_map/all_to_all | solution.py:383
  42.5 1.0 collective-permute-start.8
  43.5 0.3 neuron_gram.1.ours_ref
  43.8 3.0 %collective-permute-start.7 = (f32[128,128]{1,0:T(8,128)S(1)}, f32[128,128]{1,0:T(8,128)S(1)}, u32[]{:S(2)}, u32[]{:S(2)}) collective-permute-start(f32[128,128]{1,0:T(8,128)S(1)} %neuron_gram.1.ours_ref), channel_id=1, source_target_pairs={{0,8},{8,0},{16,24},{24,16},{32,40},{40,32},{48,56},{56,48},{64,72... | collective-permute-start | bytes 196616 | tf_op jit(solution)/shard_map/ppermute | solution.py:388
  46.8 0.9 collective-permute-done.7.theirs_ref
  47.7 13.8 %all_to_all.26.refs_0_ = f32[16,16,128]{2,1,0:T(8,128)S(1)} all-to-all(f32[16,16,128]{2,1,0:T(8,128)S(1)} %pack_gram.1), channel_id=1, replica_groups={{0,4,16,20,32,36,48,52,64,68,80,84,96,100,112,116},{1,5,17,21,33,37,49,..., dimensions={0} | all-to-all | bytes 262144 | tf_op jit(solution)/shard_map/all_to_all | solution.py:392
  61.5 0.0 collective-permute-done.8.refs_2_
  61.5 1.6 %trial_pass.1 = (f32[2048,128]{1,0:T(8,128)S(1)}, f32[128,2048]{1,0:T(8,128)S(1)}, f32[64,24,128]{2,1,0:T(8,128)S(1)}) custom-call(f32[16,16,128]{2,1,0:T(8,128)S(1)} %all_to_all.26.refs_0_, f32[1024,128]{1,0:T(8,128)S(1)} %bitcast.8, f32[1024,128]{1,0:T(8,128)S(1)} %collective-permute-done.8.refs_2_, ...), custom_call_target="tpu_custom_call" | custom-call | tf_op jit(solution)/shard_map/trial_pass/pallas_call | solution.py:393
  63.2 17.9 %all_to_all.27.gathered_ref.refs_1_ = f32[64,24,128]{2,1,0:T(8,128)S(1)} all-to-all(f32[64,24,128]{2,1,0:T(8,128)S(1)} %get-tuple-element.42), channel_id=1, replica_groups={{0,1,2,3,4,5,6,7,16,17,18,19,20,21,22,23,32,33,34,35,36,37,38,39,48,49,..., dimensions={0} | all-to-all | bytes 1572864 | tf_op jit(solution)/shard_map/all_to_all | solution.py:406
  81.1 3.2 %collective-permute-start.9 = (f32[128,128]{1,0:T(8,128)S(1)}, f32[128,128]{1,0:T(8,128)S(1)}, u32[]{:S(2)}, u32[]{:S(2)}) collective-permute-start(f32[128,128]{1,0:T(8,128)S(1)} %trial_sum.1.ours_ref), channel_id=1, source_target_pairs={{0,8},{8,0},{16,24},{24,16},{32,40},{40,32},{48,56},{56,48},{64,72... | collective-permute-start | bytes 196616 | tf_op jit(solution)/shard_map/ppermute | solution.py:408
  84.3 2.9 %second_system.1 = (f32[128,128]{1,0:T(8,128)S(1)}, f32[128,128]{1,0:T(8,128)S(1)}) custom-call(f32[128,128]{1,0:T(8,128)S(1)} %get-tuple-element.43.refs_0_, f32[64,24,128]{2,1,0:T(8,128)S(1)} %all_to_all.27.gathered_ref.refs_1_, bf16[16,1024,256]{2,1,0:T(8,128)(2,1)S(1)} %get-tuple-element.40.refs_11_.refs_2_.refs_5_.refs_0_.near_ref, ...), custom_call_target="tpu_custom_call" | custom-call | tf_op jit(solution)/shard_map/second_system/pallas_call | solution.py:409
  87.2 0.0 collective-permute-done.9.theirs_ref
  87.2 2.9 %time_pass.1 = (f32[2048,128]{1,0:T(8,128)}, f32[16,128]{1,0:T(8,128)}, f32[128,128]{1,0:T(8,128)S(1)}, f32[128,256]{1,0:T(8,128)S(1)}) custom-call(f32[128,128]{1,0:T(8,128)S(1)} %trial_sum.1.ours_ref, f32[128,128]{1,0:T(8,128)S(1)} %collective-permute-done.9.theirs_ref, f32[128,128]{1,0:T(8,128)S(1)} %get-tuple-element.44.inverse_ref, ...), custom_call_target="tpu_custom_call" | custom-call | tf_op jit(solution)/shard_map/time_pass/pallas_call | solution.py:412
  90.1 0.1 copy.7
  90.2 13.0 %all_to_all.28 = f32[128,1,256]{2,1,0:T(1,128)S(1)} all-to-all(f32[128,1,256]{2,1,0:T(1,128)S(1)} %copy.7), channel_id=1, replica_groups=mesh['neu'=16,'tri'=8] {'neu','tri'}, dimensions={0} | all-to-all | bytes 262144 | tf_op jit(solution)/shard_map/all_to_all | solution.py:429
  103.3 0.2 reduce_sum.9
  103.4 0.7 broadcast_in_dim.2
  104.2 4.3 %all-to-all-start.4 = ((f32[128,1,256]{2,1,0:T(1,128)}), f32[128,1,256]{2,1,0:T(1,128)S(1)}, u32[]{:S(2)}, u32[]{:S(2)}) async-start(f32[128,1,256]{2,1,0:T(1,128)} %broadcast_in_dim.2), calls=%async_computation.4 | async-start | bytes 262144 | tf_op jit(solution)/shard_map/all_to_all | solution.py:432
  108.4 4.4 %third_system.1.inverse_ref = f32[128,128]{1,0:T(8,128)S(1)} custom-call(f32[128,128]{1,0:T(8,128)S(1)} %get-tuple-element.50.gram_neuron_ref, f32[128,128]{1,0:T(8,128)S(1)} %get-tuple-element.51.table_ref), custom_call_target="tpu_custom_call" | custom-call | tf_op jit(solution)/shard_map/third_system/pallas_call | solution.py:430
  112.8 5.7 %all-to-all-done.4 = f32[128,1,256]{2,1,0:T(1,128)S(1)} async-done(((f32[128,1,256]{2,1,0:T(1,128)}), f32[128,1,256]{2,1,0:T(1,128)S(1)}, u32[]{:S(2)}, u32[]{:S(2)}) %all-to-all-start.4) | async-done | bytes 131104 | tf_op jit(solution)/shard_map/all_to_all | solution.py:432
  118.5 1.0 time_solve.1
  (3 shorter events, 0.1 us)
Async XLA Ops:
  5.1 14.0 %collective-permute-start = (f32[272,128]{1,0:T(8,128)S(1)}, f32[272,128]{1,0:T(8,128)S(1)}, u32[]{:S(2)}, u32[]{:S(2)}) collective-permute-start(f32[272,128]{1,0:T(8,128)S(1)} %get-tuple-element.29), channel_id=1, source_target_pairs={{0,4},{1,5},{2,6},{3,7},{4,0},{5,1},{6,2},{7,3},{8,12},{9,13},{10,... | collective-permute-start | bytes 417800 | tf_op jit(solution)/shard_map/ppermute | solution.py:366
  7.3 12.4 %collective-permute-start.1 = (f32[272,128]{1,0:T(8,128)S(1)}, f32[272,128]{1,0:T(8,128)S(1)}, u32[]{:S(2)}, u32[]{:S(2)}) collective-permute-start(f32[272,128]{1,0:T(8,128)S(1)} %get-tuple-element.30), channel_id=1, source_target_pairs={{0,5},{1,6},{2,7},{3,4},{4,1},{5,2},{6,3},{7,0},{8,13},{9,14},{10,... | collective-permute-start | bytes 417800 | tf_op jit(solution)/shard_map/ppermute | solution.py:366
  8.9 12.8 %collective-permute-start.2 = (f32[272,128]{1,0:T(8,128)S(1)}, f32[272,128]{1,0:T(8,128)S(1)}, u32[]{:S(2)}, u32[]{:S(2)}) collective-permute-start(f32[272,128]{1,0:T(8,128)S(1)} %get-tuple-element.31), channel_id=1, source_target_pairs={{0,6},{1,7},{2,4},{3,5},{4,2},{5,3},{6,0},{7,1},{8,14},{9,15},{10,... | collective-permute-start | bytes 417800 | tf_op jit(solution)/shard_map/ppermute | solution.py:366
  13.1 8.5 %collective-permute-start.3 = (f32[272,128]{1,0:T(8,128)S(1)}, f32[272,128]{1,0:T(8,128)S(1)}, u32[]{:S(2)}, u32[]{:S(2)}) collective-permute-start(f32[272,128]{1,0:T(8,128)S(1)} %get-tuple-element.32), channel_id=1, source_target_pairs={{0,7},{1,4},{2,5},{3,6},{4,3},{5,0},{6,1},{7,2},{8,15},{9,12},{10,... | collective-permute-start | bytes 417800 | tf_op jit(solution)/shard_map/ppermute | solution.py:366
  13.8 12.5 %copy-start = (bf16[256,128]{1,0:T(8,128)(2,1)S(1)}, bf16[256,128]{1,0:T(8,128)(2,1)}, u32[]{:S(2)}) copy-start(bf16[256,128]{1,0:T(8,128)(2,1)} %refs_8_.1) | copy-start | bytes 196612
  18.3 5.7 %collective-permute-start.4 = (f32[272,128]{1,0:T(8,128)S(1)}, f32[272,128]{1,0:T(8,128)S(1)}, u32[]{:S(2)}, u32[]{:S(2)}) collective-permute-start(f32[272,128]{1,0:T(8,128)S(1)} %get-tuple-element.36), channel_id=1, source_target_pairs={{0,1},{1,2},{2,3},{3,0},{4,5},{5,6},{6,7},{7,4},{8,9},{9,10},{10,1... | collective-permute-start | bytes 417800 | tf_op jit(solution)/shard_map/ppermute | solution.py:366
  19.1 6.4 %collective-permute-start.5 = (f32[272,128]{1,0:T(8,128)S(1)}, f32[272,128]{1,0:T(8,128)S(1)}, u32[]{:S(2)}, u32[]{:S(2)}) collective-permute-start(f32[272,128]{1,0:T(8,128)S(1)} %get-tuple-element.37), channel_id=1, source_target_pairs={{0,2},{1,3},{2,0},{3,1},{4,6},{5,7},{6,4},{7,5},{8,10},{9,11},{10,... | collective-permute-start | bytes 417800 | tf_op jit(solution)/shard_map/ppermute | solution.py:366
  19.6 6.6 %collective-permute-start.6 = (f32[272,128]{1,0:T(8,128)S(1)}, f32[272,128]{1,0:T(8,128)S(1)}, u32[]{:S(2)}, u32[]{:S(2)}) collective-permute-start(f32[272,128]{1,0:T(8,128)S(1)} %get-tuple-element.38), channel_id=1, source_target_pairs={{0,3},{1,0},{2,1},{3,2},{4,7},{5,4},{6,5},{7,6},{8,11},{9,8},{10,9... | collective-permute-start | bytes 417800 | tf_op jit(solution)/shard_map/ppermute | solution.py:366
  42.5 19.0 %collective-permute-start.8 = (f32[1024,128]{1,0:T(8,128)S(1)}, f32[1024,128]{1,0:T(8,128)S(1)}, u32[]{:S(2)}, u32[]{:S(2)}) collective-permute-start(f32[1024,128]{1,0:T(8,128)S(1)} %bitcast.6), channel_id=1, source_target_pairs={{0,4},{1,5},{2,6},{3,7},{4,0},{5,1},{6,2},{7,3},{8,12},{9,13},{10,... | collective-permute-start | bytes 1572872 | tf_op jit(solution)/shard_map/ppermute | solution.py:384
  43.8 3.9 %collective-permute-start.7 = (f32[128,128]{1,0:T(8,128)S(1)}, f32[128,128]{1,0:T(8,128)S(1)}, u32[]{:S(2)}, u32[]{:S(2)}) collective-permute-start(f32[128,128]{1,0:T(8,128)S(1)} %neuron_gram.1.ours_ref), channel_id=1, source_target_pairs={{0,8},{8,0},{16,24},{24,16},{32,40},{40,32},{48,56},{56,48},{64,72... | collective-permute-start | bytes 196616 | tf_op jit(solution)/shard_map/ppermute | solution.py:388
  81.1 6.1 %collective-permute-start.9 = (f32[128,128]{1,0:T(8,128)S(1)}, f32[128,128]{1,0:T(8,128)S(1)}, u32[]{:S(2)}, u32[]{:S(2)}) collective-permute-start(f32[128,128]{1,0:T(8,128)S(1)} %trial_sum.1.ours_ref), channel_id=1, source_target_pairs={{0,8},{8,0},{16,24},{24,16},{32,40},{40,32},{48,56},{56,48},{64,72... | collective-permute-start | bytes 196616 | tf_op jit(solution)/shard_map/ppermute | solution.py:408
  104.2 14.3 %all-to-all-start.4 = ((f32[128,1,256]{2,1,0:T(1,128)}), f32[128,1,256]{2,1,0:T(1,128)S(1)}, u32[]{:S(2)}, u32[]{:S(2)}) async-start(f32[128,1,256]{2,1,0:T(1,128)} %broadcast_in_dim.2), calls=%async_computation.4 | async-start | bytes 262144 | tf_op jit(solution)/shard_map/all_to_all | solution.py:432
